TPU v7x, 256 devices: a whole 4x4x8 slice. The times are simulated.
256 devices in a mesh: dp: 64 (over z_hi, y, x), tensor: 4 (over z_lo, core).
Axes of the slice: x: 4, y: 4, z: 8 (z_hi: 4, z_lo: 2; z = z_hi * 2 + z_lo), core: 2. Of those that a mesh axis runs over, the one named last changes fastest.
Arguments:
- queries: bfloat16 [64, 512, 4096], P('dp', 'tensor'), may hold values from -200 to 200
- dialogue_keys: bfloat16 [64, 512, 512], P('dp', 'tensor'), may hold values from -6 to 6
- dialogue_values: bfloat16 [64, 512, 512], P('dp', 'tensor'), may hold values from -6 to 6
- out_grad: bfloat16 [64, 512, 4096], P('dp', 'tensor'), may hold values from -96 to 96
- lengths: int32 [64], P('dp'), may hold values from 128 to 512, as said below
- cartridge: float32 [1024, 2, 512], P('dp', None, 'tensor'), may hold values from -6 to 6
- first_moment: float32 [1024, 2, 512], P('dp', None, 'tensor'), may hold values from -2 to 2
- second_moment: float32 [1024, 2, 512], P('dp', None, 'tensor'), may hold values from 0.01 to 4
Outputs:
- q_grad: bfloat16 [64, 512, 4096], P('dp', 'tensor')
- key_grad: bfloat16 [64, 512, 512], P('dp', 'tensor')
- value_grad: bfloat16 [64, 512, 512], P('dp', 'tensor')
- new_cartridge: float32 [1024, 2, 512], P('dp', None, 'tensor')
- new_m: float32 [1024, 2, 512], P('dp', None, 'tensor')
- new_v: float32 [1024, 2, 512], P('dp', None, 'tensor')
Inputs may be any that keep to these rules, and one draw needn't show every extreme that they name: `lengths`: each conversation's real tokens stand at its start; some conversation has exactly 512.
All inputs are finite; a program needn't handle non-finite values.
Results may differ from a plain program's by a relative error of at most 0.0079.
Values may be sent and summed in bfloat16 or wider, within the bound.
No kernel may reach another device: no remote copies, remote signals or barrier semaphores. Data moves between devices by JAX's collectives and lax.ppermute only.
A program may use at most 64 MiB of HBM per device.

v0:
```python
import jax
import jax.numpy as jnp
from jax import lax
from jax.sharding import PartitionSpec as P

QUERY_HEADS = 32
KEY_VALUE_HEADS = 4
HEAD_WIDTH = 128
PREFIX_TOKENS = 1024
SLOT_COUNT = 512
STEP = 10


BETA_ONE = 0.9
BETA_TWO = 0.999
ADAM_EPS = 1e-08
LEARN_RATE = 0.01
MASKED = -1e30


def dims_last(left_side, right_side):
    return lax.dot_general(
        left_side, right_side, (((1,), (1,)), ((), ())), preferred_element_type=jnp.float32
    )


def dims_first(left_side, right_side):
    return lax.dot_general(
        left_side, right_side, (((0,), (0,)), ((), ())), preferred_element_type=jnp.float32
    )


def attend_rows(row_queries, row_grads, all_keys, all_values, row_pos, score_scale):
    scores = dims_last(row_queries, all_keys) * score_scale
    key_pos = jnp.arange(all_keys.shape[0]) - PREFIX_TOKENS
    scores = jnp.where(key_pos[None, :] <= row_pos[:, None], scores, MASKED)
    row_max = jnp.max(scores, axis=1, keepdims=True)
    exp_scores = jnp.exp(scores - row_max)
    row_total = jnp.sum(exp_scores, axis=1, keepdims=True)
    weights = exp_scores / row_total
    weights_half = weights.astype(jnp.bfloat16)
    attended = jnp.dot(weights_half, all_values, preferred_element_type=jnp.float32).astype(
        jnp.bfloat16
    )
    row_dot = jnp.sum(
        row_grads.astype(jnp.float32) * attended.astype(jnp.float32), axis=1, keepdims=True
    )
    weight_grad = dims_last(row_grads, all_values)
    score_grad = (weights * (weight_grad - row_dot)).astype(jnp.bfloat16)
    return (weights_half, score_grad, row_max + jnp.log(row_total), row_dot)


def shards(
    queries,
    dialogue_keys,
    dialogue_values,
    out_grad,
    lengths,
    cartridge,
    first_moment,
    second_moment,
):
    score_scale = HEAD_WIDTH ** (-0.5)
    prefix = lax.all_gather(cartridge.astype(jnp.bfloat16), "dp", axis=0, tiled=True)
    head_queries, head_keys, head_values, head_grads = (
        lax.all_to_all(queries, "tensor", split_axis=2, concat_axis=1, tiled=True),
        lax.all_to_all(dialogue_keys, "tensor", split_axis=2, concat_axis=1, tiled=True),
        lax.all_to_all(dialogue_values, "tensor", split_axis=2, concat_axis=1, tiled=True),
        lax.all_to_all(out_grad, "tensor", split_axis=2, concat_axis=1, tiled=True),
    )
    head_group_size = QUERY_HEADS // KEY_VALUE_HEADS
    per_block = min(head_group_size, max(1, 512 // SLOT_COUNT))
    while head_group_size % per_block:
        per_block -= 1
    blocks = head_group_size // per_block
    positions = jnp.arange(SLOT_COUNT)
    row_pos = jnp.tile(positions, per_block)
    prefix_kparts = [jnp.zeros((PREFIX_TOKENS, HEAD_WIDTH), jnp.float32)]
    prefix_vparts = [jnp.zeros((PREFIX_TOKENS, HEAD_WIDTH), jnp.float32)]
    query_rows, key_rows, value_rows = ([], [], [])
    is_real = positions < lengths[0]
    sample_grads = jnp.where(is_real[:, None], head_grads[0], jnp.zeros((), head_grads.dtype))
    columns = slice(0, HEAD_WIDTH)
    all_keys = jnp.concatenate([prefix[:, 0, columns], head_keys[0]], 0)
    all_values = jnp.concatenate([prefix[:, 1, columns], head_values[0]], 0)
    query_blocks = (
        head_queries[0]
        .reshape(SLOT_COUNT, blocks, per_block, HEAD_WIDTH)
        .transpose(1, 2, 0, 3)
        .reshape(blocks, per_block * SLOT_COUNT, HEAD_WIDTH)
    )
    grad_blocks = (
        sample_grads.reshape(SLOT_COUNT, blocks, per_block, HEAD_WIDTH)
        .transpose(1, 2, 0, 3)
        .reshape(blocks, per_block * SLOT_COUNT, HEAD_WIDTH)
    )

    def block_step(running, inputs, all_keys=all_keys, all_values=all_values):
        row_queries, row_grads = inputs
        weights_half, score_grad, log_total, row_dot = attend_rows(
            row_queries, row_grads, all_keys, all_values, row_pos, score_scale
        )
        query_grad = (
            jnp.dot(score_grad, all_keys, preferred_element_type=jnp.float32) * score_scale
        ).astype(jnp.bfloat16)
        key_more = dims_first(score_grad, row_queries) * score_scale
        value_more = dims_first(weights_half, row_grads)
        return ((running[0] + key_more, running[1] + value_more), (query_grad, log_total, row_dot))

    empty_rows = jnp.zeros((PREFIX_TOKENS + SLOT_COUNT, HEAD_WIDTH), jnp.float32)
    (key_sum, value_sum), (query_blocks_grad, log_totals, row_dots) = lax.scan(
        block_step, (empty_rows, empty_rows), (query_blocks, grad_blocks)
    )
    query_parts = (
        query_blocks_grad.reshape(blocks, per_block, SLOT_COUNT, HEAD_WIDTH)
        .transpose(2, 0, 1, 3)
        .reshape(SLOT_COUNT, head_group_size * HEAD_WIDTH)
    )
    key_parts = key_sum[-SLOT_COUNT:].astype(jnp.bfloat16)
    value_parts = value_sum[-SLOT_COUNT:].astype(jnp.bfloat16)
    prefix_kparts[0] = key_sum[:PREFIX_TOKENS]
    prefix_vparts[0] = value_sum[:PREFIX_TOKENS]
    query_rows.append(query_parts)
    key_rows.append(key_parts)
    value_rows.append(value_parts)
    q_grad, key_grad, value_grad = (
        lax.all_to_all(jnp.stack(query_rows, 0), "tensor", split_axis=1, concat_axis=2, tiled=True),
        lax.all_to_all(jnp.stack(key_rows, 0), "tensor", split_axis=1, concat_axis=2, tiled=True),
        lax.all_to_all(jnp.stack(value_rows, 0), "tensor", split_axis=1, concat_axis=2, tiled=True),
    )
    local_grads = jnp.stack([prefix_kparts[0], prefix_vparts[0]], 1)
    prefix_grad = lax.psum_scatter(local_grads, "dp", scatter_dimension=0, tiled=True)
    new_m = BETA_ONE * first_moment + (1.0 - BETA_ONE) * prefix_grad
    new_v = BETA_TWO * second_moment + (1.0 - BETA_TWO) * prefix_grad * prefix_grad
    update = new_m / (1.0 - BETA_ONE**STEP) / (jnp.sqrt(new_v / (1.0 - BETA_TWO**STEP)) + ADAM_EPS)
    new_cartridge = cartridge - LEARN_RATE * update
    return (q_grad, key_grad, value_grad, new_cartridge, new_m, new_v)


def solution(mesh):
    in_specs = (
        P("dp", "tensor", None),
        P("dp", "tensor", None),
        P("dp", "tensor", None),
        P("dp", "tensor", None),
        P("dp"),
        P("dp", None, "tensor"),
        P("dp", None, "tensor"),
        P("dp", None, "tensor"),
    )
    out_specs = (
        P("dp", "tensor", None),
        P("dp", "tensor", None),
        P("dp", "tensor", None),
        P("dp", None, "tensor"),
        P("dp", None, "tensor"),
        P("dp", None, "tensor"),
    )
    return jax.shard_map(shards, mesh=mesh, in_specs=in_specs, out_specs=out_specs, check_vma=False)
```

profile of v0, /device:TPU:2, one launch (start us, length us, event | category | flops | bytes accessed | tf_op | source)
XLA Modules:
  0.0 1228.8 jit_solution(9534744803625573890)
XLA Ops:
  11.0 3.3 all-to-all-start.3
  19.5 3.3 all-to-all-start.1
  22.9 2.8 copy.76
  25.7 22.4 %reduce.3 = bf16[4096,128]{1,0:T(8,128)(2,1)S(1)} reduce(bf16[4096,1,128]{2,1,0:T(2,128)(2,1)S(1)} %bitcast.131, bf16[]{:T(256)} %broadcast.76), dimensions={1}, to_apply=%bitcast.80.reduce_sub_computation | reduce | bytes 2097154
  49.8 3.7 all-to-all-start.2
  53.5 5.0 copy.71
  58.6 23.4 %reduce = bf16[4096,128]{1,0:T(8,128)(2,1)} reduce(bf16[4096,1,128]{2,1,0:T(2,128)(2,1)S(1)} %bitcast.132, bf16[]{:T(256)} %broadcast.76), dimensions={1}, to_apply=%bitcast.76.reduce_sub_computation | reduce | bytes 2097154
  81.9 3.5 reshape.57
  86.5 3.5 all-to-all-start
  91.2 199.3 %all_gather.3 = bf16[1024,2,128]{2,0,1:T(8,128)(2,1)S(1)} all-gather(bf16[16,2,128]{2,0,1:T(8,128)(2,1)S(1)} %copy.104), channel_id=1, replica_groups=mesh['dp'=64,'tensor'=4] {'dp'}, dimensions={0}, use_global_device_ids=true | all-gather | bytes 532480 | tf_op jit(solution)/shard_map/all_gather | solution.py:64
  304.3 149.0 %while.17 = (s32[]{:T(128)}, f32[1536,128]{1,0:T(8,128)}, f32[1536,128]{1,0:T(8,128)}, bf16[8,512,128]{1,2,0:T(8,128)(2,1)}, bf16[8,512,128]{2,1,0:T(8,128)(2,1)...) while((s32[]{:T(128)}, f32[1536,128]{1,0:T(8,128)}, ...), condition=%wide.region_4.5_spmd.clone, body=%wide.region_0.4_spmd.clone.sunk | while | flops 1219624960 | bytes 39088780 | solution.py:111
  317.1 2.9 fusion.72
  335.3 3.1 fusion.72
  338.4 2.7 convolution_add_fusion.2
  354.0 3.1 fusion.72
  357.1 2.7 convolution_add_fusion.2
  372.7 3.1 fusion.72
  375.8 2.7 convolution_add_fusion.2
  391.4 3.1 fusion.72
  394.5 2.7 convolution_add_fusion.2
  410.1 3.1 fusion.72
  413.2 2.7 convolution_add_fusion.2
  428.8 3.1 fusion.72
  431.9 2.7 convolution_add_fusion.2
  447.5 3.1 fusion.72
  456.6 3.3 all-to-all-start.5
  464.5 3.6 all-to-all-start.6
  468.1 4.7 copy.83
  472.9 7.8 reduce.4
  480.7 3.7 reshape.65
  484.4 3.5 all-to-all-start.4
  494.5 722.7 %all-reduce.3.cloned.1.call-done = f32[1024,2,128]{2,1,0:T(2,128)} async-done(((f32[1024,2,128]{2,1,0:T(2,128)}), f32[1024,2,128]{2,1,0:T(2,128)}) %all-reduce.3.cloned.1.call-update) | async-done | bytes 1048592
  (178 shorter events, 151.9 us)
Async XLA Ops:
  7.2 15.7 %copy-start.3 = (bf16[1,128,4096]{2,1,0:T(8,128)(2,1)S(1)}, bf16[1,128,4096]{2,1,0:T(8,128)(2,1)}, u32[]{:S(2)}) copy-start(bf16[1,128,4096]{2,1,0:T(8,128)(2,1)} %param.13) | copy-start | bytes 3145732
  11.0 7.9 all-to-all-start.3
  18.9 0.7 copy-start.4
  19.5 30.3 %all-to-all-start.1 = ((bf16[4,2,8192]{2,1,0:T(2,128)(2,1)}), bf16[4,2,8192]{2,1,0:T(2,128)(2,1)S(1)}, u32[]{:S(2)}, u32[]{:S(2)}) async-start(bf16[4,2,8192]{2,1,0:T(2,128)(2,1)} %reshape.59), calls=%async_computation.1 | async-start | bytes 262144 | tf_op jit(solution)/shard_map/all_to_all | solution.py:67
  49.8 32.1 %copy-start.6 = (bf16[4,2,8192]{2,1,0:T(2,128)(2,1)}, bf16[4,2,8192]{2,1,0:T(2,128)(2,1)S(1)}, u32[]{:S(2)}) copy-start(bf16[4,2,8192]{2,1,0:T(2,128)(2,1)S(1)} %all-to-all-done.1) | copy-start | bytes 393220
  49.8 35.6 %all-to-all-start.2 = ((bf16[4,2,65536]{2,1,0:T(2,128)(2,1)}), bf16[4,2,65536]{2,1,0:T(2,128)(2,1)S(1)}, u32[]{:S(2)}, u32[]{:S(2)}) async-start(bf16[4,2,65536]{2,1,0:T(2,128)(2,1)} %reshape.61), calls=%async_computation.2 | async-start | bytes 2097152 | tf_op jit(solution)/shard_map/all_to_all | solution.py:69
  58.6 31.5 %copy-start.8 = (f32[16,2,128]{2,1,0:T(2,128)S(1)}, f32[16,2,128]{2,1,0:T(2,128)}, u32[]{:S(2)}) copy-start(f32[16,2,128]{2,1,0:T(2,128)} %param.15) | copy-start | bytes 49156
  81.9 208.6 %copy-start.5 = (bf16[4,2,8192]{2,1,0:T(2,128)(2,1)S(1)}, bf16[4,2,8192]{2,1,0:T(2,128)(2,1)}, u32[]{:S(2)}) copy-start(bf16[4,2,8192]{2,1,0:T(2,128)(2,1)} %copy-done.4) | copy-start | bytes 393220
  85.4 205.4 %copy-start.7 = (bf16[4,2,8192]{2,1,0:T(2,128)(2,1)S(1)}, bf16[4,2,8192]{2,1,0:T(2,128)(2,1)}, u32[]{:S(2)}) copy-start(bf16[4,2,8192]{2,1,0:T(2,128)(2,1)} %copy-done.6) | copy-start | bytes 393220
  85.4 1.0 copy-start.2
  86.5 214.7 %all-to-all-start = ((bf16[4,2,65536]{2,1,0:T(2,128)(2,1)}), bf16[4,2,65536]{2,1,0:T(2,128)(2,1)S(1)}, u32[]{:S(2)}, u32[]{:S(2)}) async-start(bf16[4,2,65536]{2,1,0:T(2,128)(2,1)} %reshape.57), calls=%async_computation | async-start | bytes 2097152 | tf_op jit(solution)/shard_map/all_to_all | solution.py:66
  310.5 1.2 copy-start
  328.7 1.2 copy-start
  347.4 1.2 copy-start
  366.1 1.2 copy-start
  384.8 1.2 copy-start
  403.5 1.2 copy-start
  422.1 1.2 copy-start
  440.8 1.2 copy-start
  456.6 7.9 all-to-all-start.5
  464.5 19.9 %all-to-all-start.6 = ((bf16[4,2,8192]{2,1,0:T(2,128)(2,1)}), bf16[4,2,8192]{2,1,0:T(2,128)(2,1)S(1)}, u32[]{:S(2)}, u32[]{:S(2)}) async-start(bf16[4,2,8192]{2,1,0:T(2,128)(2,1)} %reshape.69), calls=%async_computation.6 | async-start | bytes 262144 | tf_op jit(solution)/shard_map/all_to_all | solution.py:129
  472.9 15.1 %copy-start.1 = (f32[1536,128]{1,0:T(8,128)S(1)}, f32[1536,128]{1,0:T(8,128)}, u32[]{:S(2)}) copy-start(f32[1536,128]{1,0:T(8,128)} %get-tuple-element.122) | copy-start | bytes 2359300
  484.4 734.2 %all-to-all-start.4 = ((bf16[4,2,65536]{2,1,0:T(2,128)(2,1)}), bf16[4,2,65536]{2,1,0:T(2,128)(2,1)S(1)}, u32[]{:S(2)}, u32[]{:S(2)}) async-start(bf16[4,2,65536]{2,1,0:T(2,128)(2,1)} %reshape.65), calls=%async_computation.4 | async-start | bytes 2097152 | tf_op jit(solution)/shard_map/all_to_all | solution.py:127
  487.9 3.2 copy-start.11
  488.0 729.3 %all-reduce.3.cloned.1.call-start = ((), (), s32[]{:S(2)}) async-start(), calls=%async_computation.7 | async-start | bytes 2097152
  489.1 728.1 %copy-start.9 = (f32[16,2,128]{2,1,0:T(2,128)S(1)}, f32[16,2,128]{2,1,0:T(2,128)}, u32[]{:S(2)}) copy-start(f32[16,2,128]{2,1,0:T(2,128)} %param.16) | copy-start | bytes 49156
  489.2 728.1 %copy-start.10 = (f32[16,2,128]{2,1,0:T(2,128)S(1)}, f32[16,2,128]{2,1,0:T(2,128)}, u32[]{:S(2)}) copy-start(f32[16,2,128]{2,1,0:T(2,128)} %param.17) | copy-start | bytes 49156
Sparse Core Ops, SparseCore 0:
  492.0 725.2 all-reduce.2
where the time goes:
time: 1230 us
  waiting for transfers between devices  725 us (59%)
  blocking collectives  199 us (16%)
  matrix products  104 us (8%)
  local copies, waits for them, and re-layouts  83.9 us (7%)
  other arithmetic  76 us (6%)
  starting transfers between devices  24.3 us (2%)
  between operations  15.8 us (1%)
    unnamed x2, waiting for transfers between devices  723 us
    all_gather x1, blocking collectives, shards(): lax.all_gather(cartridge.astype(jnp.bfloat16), 'dp', axis=0, tiled=True)  199 us
    unnamed x9, other arithmetic  59.2 us
    dot_general x16, matrix products, dims_first(): lax.dot_general(left_side, right_side, (((0,), (0,)), ((), ())), preferre...  46.2 us
    unnamed x57, local copies, waits for them, and re-layouts  37.4 us
    dot_general x16, matrix products, dims_last(): lax.dot_general(left_side, right_side, (((1,), (1,)), ((), ())), preferre...  27.1 us
    dynamic_update_slice x16, local copies, waits for them, and re-layouts, shards(): lax.scan(block_step, (empty_rows, empty_rows), (query_blocks, grad_blocks))  25.8 us
  transfers between devices with their start and end apart: 8, of which 3 were waited for; matrix products, arithmetic and copies ran while one was open for 8% of the time, Pallas kernels for 0%

commit v1 on v0

v1 whole, which is shorter than its diff:
```python
import jax
import jax.numpy as jnp
from jax import lax
from jax.experimental import pallas as pl
from jax.experimental.pallas import tpu as pltpu
from jax.sharding import PartitionSpec as P

QUERY_HEADS = 32
KEY_VALUE_HEADS = 4
HEAD_WIDTH = 128
PREFIX_TOKENS = 1024
SLOT_COUNT = 512
STEP = 10

BETA_ONE = 0.9
BETA_TWO = 0.999
ADAM_EPS = 1e-08
LEARN_RATE = 0.01
MASKED = -1e30
GROUP = QUERY_HEADS // KEY_VALUE_HEADS
ALL_TOKENS = PREFIX_TOKENS + SLOT_COUNT
SCALE = HEAD_WIDTH ** (-0.5)
LOG2_SCALE = SCALE * 1.4426950408889634

ROWS = 256
CHUNK = 256
BLOCKS = SLOT_COUNT // ROWS

bf16 = jnp.bfloat16
f32 = jnp.float32


def nn(a, b):
    return jnp.dot(a, b, preferred_element_type=f32)


def nt(a, b):
    return lax.dot_general(a, b, (((1,), (1,)), ((), ())), preferred_element_type=f32)


def turned(a):
    return a.astype(f32).T


def attention_kernel(
    length_ref, q_ref, g_ref, kv_ref, prefix_ref, qgrad_ref, kvgrad_ref, pgrad_ref,
    keys, values, keys_t, values_t, dkeys, dvalues, exps,
):
    head = pl.program_id(0)
    length = length_ref[0]

    @pl.when(head == 0)
    def _():
        keys[:PREFIX_TOKENS] = prefix_ref[:, :HEAD_WIDTH]
        keys[PREFIX_TOKENS:] = kv_ref[:, :HEAD_WIDTH]
        values[:PREFIX_TOKENS] = prefix_ref[:, HEAD_WIDTH:]
        values[PREFIX_TOKENS:] = kv_ref[:, HEAD_WIDTH:]
        for start in range(0, ALL_TOKENS, CHUNK):
            span = slice(start, start + CHUNK)
            keys_t[:, span] = turned(keys[span]).astype(bf16)
            values_t[:, span] = turned(values[span]).astype(bf16)
        dkeys[...] = jnp.zeros_like(dkeys)
        dvalues[...] = jnp.zeros_like(dvalues)

    for block in range(BLOCKS):
        first = block * ROWS
        rows = slice(first, first + ROWS)
        spans = [slice(s, s + CHUNK) for s in range(0, PREFIX_TOKENS + first + ROWS, CHUNK)]
        q = q_ref[rows]
        row_index = first + lax.broadcasted_iota(jnp.int32, (ROWS, HEAD_WIDTH), 0)
        g = jnp.where(row_index < length, g_ref[rows], jnp.zeros((), bf16))
        g_t = turned(g)
        top = None
        for span in spans:
            scores = nt(keys[span], q)
            if span.stop > PREFIX_TOKENS + first:
                key_pos = span.start - PREFIX_TOKENS + lax.broadcasted_iota(jnp.int32, (CHUNK, ROWS), 0)
                row_pos = first + lax.broadcasted_iota(jnp.int32, (CHUNK, ROWS), 1)
                scores = jnp.where(key_pos <= row_pos, scores, MASKED)
            exps[block, span] = scores
            chunk_top = jnp.max(scores, axis=0, keepdims=True)
            top = chunk_top if top is None else jnp.maximum(top, chunk_top)
        total = jnp.zeros((1, ROWS), f32)
        for span in spans:
            e = jnp.exp2((exps[block, span] - top) * LOG2_SCALE)
            exps[block, span] = e
            total = total + jnp.sum(e, axis=0, keepdims=True)
        inverse = 1.0 / total
        attended_t = jnp.zeros((HEAD_WIDTH, ROWS), f32)
        for span in spans:
            weights = exps[block, span] * inverse
            exps[block, span] = weights
            half = weights.astype(bf16)
            attended_t = attended_t + nn(values_t[:, span], half)
            dvalues[span] += nn(half, g)
        row_dot = jnp.sum(g_t * attended_t.astype(bf16).astype(f32), axis=0, keepdims=True)
        qgrad_t = jnp.zeros((HEAD_WIDTH, ROWS), f32)
        for span in spans:
            weight_grad = nt(values[span], g)
            score_grad = (exps[block, span] * (weight_grad - row_dot)).astype(bf16)
            qgrad_t = qgrad_t + nn(keys_t[:, span], score_grad)
            dkeys[span] += nn(score_grad, q)
        qgrad_ref[rows] = (qgrad_t * SCALE).T.astype(bf16)

    @pl.when(head == GROUP - 1)
    def _():
        pgrad_ref[:, :HEAD_WIDTH] = (dkeys[:PREFIX_TOKENS] * SCALE).astype(bf16)
        pgrad_ref[:, HEAD_WIDTH:] = dvalues[:PREFIX_TOKENS].astype(bf16)
        kvgrad_ref[:, :HEAD_WIDTH] = (dkeys[PREFIX_TOKENS:] * SCALE).astype(bf16)
        kvgrad_ref[:, HEAD_WIDTH:] = dvalues[PREFIX_TOKENS:].astype(bf16)


def attention(length, tokens, prefix):
    return pl.pallas_call(
        attention_kernel,
        grid=(GROUP,),
        in_specs=[
            pl.BlockSpec(memory_space=pltpu.SMEM),
            pl.BlockSpec((SLOT_COUNT, HEAD_WIDTH), lambda h: (0, h)),
            pl.BlockSpec((SLOT_COUNT, HEAD_WIDTH), lambda h: (0, GROUP + h)),
            pl.BlockSpec((SLOT_COUNT, 2 * HEAD_WIDTH), lambda h: (0, GROUP)),
            pl.BlockSpec((PREFIX_TOKENS, 2 * HEAD_WIDTH), lambda h: (0, 0)),
        ],
        out_specs=[
            pl.BlockSpec((SLOT_COUNT, HEAD_WIDTH), lambda h: (0, h)),
            pl.BlockSpec((SLOT_COUNT, 2 * HEAD_WIDTH), lambda h: (0, 0)),
            pl.BlockSpec((PREFIX_TOKENS, 2 * HEAD_WIDTH), lambda h: (0, 0)),
        ],
        out_shape=[
            jax.ShapeDtypeStruct((SLOT_COUNT, GROUP * HEAD_WIDTH), bf16),
            jax.ShapeDtypeStruct((SLOT_COUNT, 2 * HEAD_WIDTH), bf16),
            jax.ShapeDtypeStruct((PREFIX_TOKENS, 2 * HEAD_WIDTH), bf16),
        ],
        scratch_shapes=[
            pltpu.VMEM((ALL_TOKENS, HEAD_WIDTH), bf16),
            pltpu.VMEM((ALL_TOKENS, HEAD_WIDTH), bf16),
            pltpu.VMEM((HEAD_WIDTH, ALL_TOKENS), bf16),
            pltpu.VMEM((HEAD_WIDTH, ALL_TOKENS), bf16),
            pltpu.VMEM((ALL_TOKENS, HEAD_WIDTH), f32),
            pltpu.VMEM((ALL_TOKENS, HEAD_WIDTH), f32),
            pltpu.VMEM((BLOCKS, ALL_TOKENS, ROWS), f32),
        ],
        compiler_params=pltpu.CompilerParams(
            dimension_semantics=("arbitrary",), vmem_limit_bytes=40 * 1024 * 1024
        ),
        cost_estimate=pl.CostEstimate(flops=9 * 10**9, bytes_accessed=5 * 10**6, transcendentals=6 * 10**6),
    )(length, tokens, tokens, tokens, prefix)


def shards(
    queries,
    dialogue_keys,
    dialogue_values,
    out_grad,
    lengths,
    cartridge,
    first_moment,
    second_moment,
):
    tensor_size = lax.axis_size("tensor")
    dp_size = lax.axis_size("dp")
    own_rows = SLOT_COUNT // tensor_size
    head_columns = GROUP * HEAD_WIDTH

    own_prefix = cartridge.astype(bf16).reshape(PREFIX_TOKENS // dp_size, 2 * HEAD_WIDTH)
    prefix = lax.all_to_all(
        jnp.broadcast_to(own_prefix[None], (dp_size,) + own_prefix.shape), "dp", 0, 0
    ).reshape(PREFIX_TOKENS, 2 * HEAD_WIDTH)

    outgoing = jnp.stack(
        [
            jnp.concatenate(
                [
                    queries[0, :, t * head_columns : (t + 1) * head_columns],
                    out_grad[0, :, t * head_columns : (t + 1) * head_columns],
                    dialogue_keys[0, :, t * HEAD_WIDTH : (t + 1) * HEAD_WIDTH],
                    dialogue_values[0, :, t * HEAD_WIDTH : (t + 1) * HEAD_WIDTH],
                ],
                1,
            )
            for t in range(tensor_size)
        ]
    )
    tokens = lax.all_to_all(outgoing, "tensor", 0, 0).reshape(SLOT_COUNT, -1)

    query_grad, kv_grad, prefix_part = attention(lengths, tokens, prefix)

    arrived = lax.all_to_all(
        prefix_part.reshape(dp_size, PREFIX_TOKENS // dp_size, 2 * HEAD_WIDTH), "dp", 0, 0
    )
    returned = lax.all_to_all(
        jnp.concatenate([query_grad, kv_grad], 1).reshape(tensor_size, own_rows, -1), "tensor", 0, 0
    )
    q_grad = jnp.concatenate([returned[t, :, :head_columns] for t in range(tensor_size)], 1)[None]
    key_grad = jnp.concatenate(
        [returned[t, :, head_columns : head_columns + HEAD_WIDTH] for t in range(tensor_size)], 1
    )[None]
    value_grad = jnp.concatenate(
        [returned[t, :, head_columns + HEAD_WIDTH :] for t in range(tensor_size)], 1
    )[None]

    prefix_grad = jnp.sum(arrived.astype(f32), 0).reshape(cartridge.shape)
    new_m = BETA_ONE * first_moment + (1.0 - BETA_ONE) * prefix_grad
    new_v = BETA_TWO * second_moment + (1.0 - BETA_TWO) * prefix_grad * prefix_grad
    update = new_m / (1.0 - BETA_ONE**STEP) / (jnp.sqrt(new_v / (1.0 - BETA_TWO**STEP)) + ADAM_EPS)
    new_cartridge = cartridge - LEARN_RATE * update
    return (q_grad, key_grad, value_grad, new_cartridge, new_m, new_v)


def solution(mesh):
    tokens = P("dp", "tensor", None)
    trained = P("dp", None, "tensor")
    return jax.shard_map(
        shards,
        mesh=mesh,
        in_specs=(tokens, tokens, tokens, tokens, P("dp"), trained, trained, trained),
        out_specs=(tokens, tokens, tokens, trained, trained, trained),
        check_vma=False,
    )
```

time: 1230 us -> 156 us (0.13)
  the two profiles are of different devices: /device:TPU:2 before, /device:TPU:1 now
where the time goes in v1:
time: 156 us
  waiting for transfers between devices  72 us (46%)
  starting transfers between devices  34.9 us (22%)
  Pallas kernels  33.6 us (22%)
  other arithmetic  7.05 us (5%)
  local copies, waits for them, and re-layouts  6.55 us (4%)
    pallas_call x1, Pallas kernels, attention(): pl.pallas_call(attention_kernel, grid=(GROUP,), in_specs=[pl.BlockSpec(me...  33.6 us
    all_to_all x1, waiting for transfers between devices, shards(): tokens = lax.all_to_all(outgoing, 'tensor', 0, 0).reshape(SLOT_COUNT, -1)  27 us
    all_to_all x1, waiting for transfers between devices, shards(): lax.all_to_all(prefix_part.reshape(dp_size, PREFIX_TOKENS // dp_size, 2 *...  16.7 us
    all_to_all x1, waiting for transfers between devices, shards(): lax.all_to_all(jnp.concatenate([query_grad, kv_grad], 1).reshape(tensor_s...  15.6 us
    all_to_all x1, starting transfers between devices, shards(): lax.all_to_all(jnp.broadcast_to(own_prefix[None], (dp_size,) + own_prefix...  15.1 us
    all_to_all x1, waiting for transfers between devices, shards(): lax.all_to_all(jnp.broadcast_to(own_prefix[None], (dp_size,) + own_prefix...  12.7 us
    all_to_all x1, starting transfers between devices, shards(): tokens = lax.all_to_all(outgoing, 'tensor', 0, 0).reshape(SLOT_COUNT, -1)  7.62 us
    all_to_all x1, starting transfers between devices, shards(): lax.all_to_all(jnp.concatenate([query_grad, kv_grad], 1).reshape(tensor_s...  6.51 us
  transfers between devices with their start and end apart: 4, of which 4 were waited for; matrix products, arithmetic and copies ran while one was open for 3% of the time, Pallas kernels for 0%

profile of v1, /device:TPU:1, one launch (start us, length us, event | category | flops | bytes accessed | tf_op | source)
XLA Modules:
  0.0 155.5 jit_solution(9061511821189830249)
XLA Ops:
  0.6 0.8 convert_element_type.6
  1.5 0.8 broadcast_in_dim.17
  2.3 15.1 %all-to-all-start.1 = ((bf16[64,16,256]{2,1,0:T(8,128)(2,1)}), bf16[64,16,256]{2,1,0:T(8,128)(2,1)S(1)}, u32[]{:S(2)}, u32[]{:S(2)}) async-start(bf16[64,16,256]{2,1,0:T(8,128)(2,1)} %broadcast_in_dim.17), calls=%async_computation.1 | async-start | bytes 1048576 | tf_op jit(solution)/shard_map/all_to_all | solution.py:166
  17.4 0.0 copy-start.6
  17.4 0.1 slice_bitcast_fusion.11
  17.5 1.1 copy-done.6
  18.7 0.1 slice_bitcast_fusion.10
  18.7 0.8 copy-done.7
  19.6 0.0 copy-done.8
  19.6 0.1 maximum_bitcast_fusion.1
  19.7 0.1 maximum_bitcast_fusion.3
  19.8 1.7 %pad_maximum_fusion = bf16[4,128,2304]{2,1,0:T(8,128)(2,1)} fusion(bf16[1,128,2304]{2,1,0:T(8,128)(2,1)S(1)} %get-tuple-element.46, bf16[1,128,2304]{2,1,0:T(8,128)(2,1)S(1)} %get-tuple-element.45, bf16[1,128,2304]{2,1,0:T(8,128)(2,1)S(1)} %get-tuple-element.44, bf16[1,128,2304]{2,1,0:T(8,128)(2,1)S(1)} %get-tuple-element.43), kind=kLoop, calls=%fused_computation | loop fusion | flops 3538944 | bytes 4718592 | tf_op jit(solution)/shard_map/stack | solution.py:170
  21.6 12.7 %all-to-all-done.1 = bf16[64,16,256]{2,1,0:T(8,128)(2,1)S(1)} async-done(((bf16[64,16,256]{2,1,0:T(8,128)(2,1)}), bf16[64,16,256]{2,1,0:T(8,128)(2,1)S(1)}, u32[]{:S(2)}, u32[]{:S(2)}) %all-to-all-start.1) | async-done | bytes 524320 | tf_op jit(solution)/shard_map/all_to_all | solution.py:166
  34.3 0.8 copy-done
  35.1 7.6 %all-to-all-start = ((bf16[4,128,2304]{2,1,0:T(8,128)(2,1)}), bf16[4,128,2304]{2,1,0:T(8,128)(2,1)S(1)}, u32[]{:S(2)}, u32[]{:S(2)}) async-start(bf16[4,128,2304]{2,1,0:T(8,128)(2,1)} %pad_maximum_fusion), calls=%async_computation | async-start | bytes 4718592 | tf_op jit(solution)/shard_map/all_to_all | solution.py:184
  43.4 27.0 %all-to-all-done = bf16[4,128,2304]{2,1,0:T(8,128)(2,1)S(1)} async-done(((bf16[4,128,2304]{2,1,0:T(8,128)(2,1)}), bf16[4,128,2304]{2,1,0:T(8,128)(2,1)S(1)}, u32[]{:S(2)}, u32[]{:S(2)}) %all-to-all-start) | async-done | bytes 2359328 | tf_op jit(solution)/shard_map/all_to_all | solution.py:184
  70.4 1.0 copy-done.1
  71.4 33.6 %shard_map.127 = (bf16[512,1024]{1,0:T(8,128)(2,1)S(1)}, bf16[512,256]{1,0:T(8,128)(2,1)S(1)}, bf16[1024,256]{1,0:T(8,128)(2,1)S(1)}) custom-call(s32[1]{0:T(128)S(6)} %copy.17.length_ref, bf16[512,2304]{1,0:T(8,128)(2,1)S(1)} %bitcast.78, bf16[512,2304]{1,0:T(8,128)(2,1)S(1)} %bitcast.79, bf16[512,2304]{1,0:T(8,128)(2,1)S(1)} %bitcast.80, ...), custom_call_target="tpu_custom_call" | custom-call | flops 8999999488 | bytes 5000000 | tf_op jit(solution)/shard_map/pallas_call | solution.py:114
  105.0 0.0 copy-start.2
  105.0 0.8 copy-done.2
  105.8 0.7 copy-done.3
  106.5 5.7 %all-to-all-start.3 = ((bf16[64,16,256]{2,1,0:T(8,128)(2,1)}), bf16[64,16,256]{2,1,0:T(8,128)(2,1)S(1)}, u32[]{:S(2)}, u32[]{:S(2)}) async-start(bf16[64,16,256]{2,1,0:T(8,128)(2,1)} %bitcast.82), calls=%async_computation.3 | async-start | bytes 1048576 | tf_op jit(solution)/shard_map/all_to_all | solution.py:188
  112.2 1.2 pad_maximum_fusion.1
  113.3 16.7 %all-to-all-done.3 = bf16[64,16,256]{2,1,0:T(8,128)(2,1)S(1)} async-done(((bf16[64,16,256]{2,1,0:T(8,128)(2,1)}), bf16[64,16,256]{2,1,0:T(8,128)(2,1)S(1)}, u32[]{:S(2)}, u32[]{:S(2)}) %all-to-all-start.3) | async-done | bytes 524320 | tf_op jit(solution)/shard_map/all_to_all | solution.py:188
  130.0 6.5 %all-to-all-start.2 = ((bf16[4,128,1280]{2,1,0:T(8,128)(2,1)}), bf16[4,128,1280]{2,1,0:T(8,128)(2,1)S(1)}, u32[]{:S(2)}, u32[]{:S(2)}) async-start(bf16[4,128,1280]{2,1,0:T(8,128)(2,1)} %bitcast.22), calls=%async_computation.2 | async-start | bytes 2621440 | tf_op jit(solution)/shard_map/all_to_all | solution.py:191
  136.5 0.1 convert_reduce_fusion
  136.7 0.7 multiply_subtract_fusion
  137.3 15.6 %all-to-all-done.2 = bf16[4,128,1280]{2,1,0:T(8,128)(2,1)S(1)} async-done(((bf16[4,128,1280]{2,1,0:T(8,128)(2,1)}), bf16[4,128,1280]{2,1,0:T(8,128)(2,1)S(1)}, u32[]{:S(2)}, u32[]{:S(2)}) %all-to-all-start.2) | async-done | bytes 1310752 | tf_op jit(solution)/shard_map/all_to_all | solution.py:191
  153.0 0.7 maximum_bitcast_fusion.6
  153.7 0.7 maximum_bitcast_fusion.5
  154.3 0.1 slice_bitcast_fusion.3
  154.5 1.0 maximum_bitcast_fusion
  (20 shorter events, 0.1 us)
Async XLA Ops:
  0.6 16.8 %copy-start.5 = (bf16[1,128,4096]{2,1,0:T(8,128)(2,1)S(1)}, bf16[1,128,4096]{2,1,0:T(8,128)(2,1)}, u32[]{:S(2)}) copy-start(bf16[1,128,4096]{2,1,0:T(8,128)(2,1)} %param.8) | copy-start | bytes 3145732
  2.3 32.0 %all-to-all-start.1 = ((bf16[64,16,256]{2,1,0:T(8,128)(2,1)}), bf16[64,16,256]{2,1,0:T(8,128)(2,1)S(1)}, u32[]{:S(2)}, u32[]{:S(2)}) async-start(bf16[64,16,256]{2,1,0:T(8,128)(2,1)} %broadcast_in_dim.17), calls=%async_computation.1 | async-start | bytes 1048576 | tf_op jit(solution)/shard_map/all_to_all | solution.py:166
  17.4 1.2 copy-start.6
  18.7 0.9 copy-start.7
  18.7 1.0 copy-start.8
  34.3 0.8 copy-start
  35.1 35.3 %all-to-all-start = ((bf16[4,128,2304]{2,1,0:T(8,128)(2,1)}), bf16[4,128,2304]{2,1,0:T(8,128)(2,1)S(1)}, u32[]{:S(2)}, u32[]{:S(2)}) async-start(bf16[4,128,2304]{2,1,0:T(8,128)(2,1)} %pad_maximum_fusion), calls=%async_computation | async-start | bytes 4718592 | tf_op jit(solution)/shard_map/all_to_all | solution.py:184
  70.4 1.0 copy-start.1
  105.0 0.8 copy-start.2
  105.8 0.7 copy-start.3
  106.5 5.7 %copy-start.4 = (bf16[512,256]{1,0:T(8,128)(2,1)S(1)}, bf16[512,256]{1,0:T(8,128)(2,1)}, u32[]{:S(2)}) copy-start(bf16[512,256]{1,0:T(8,128)(2,1)} %copy-done.3) | copy-start | bytes 786436
  106.5 23.5 %all-to-all-start.3 = ((bf16[64,16,256]{2,1,0:T(8,128)(2,1)}), bf16[64,16,256]{2,1,0:T(8,128)(2,1)S(1)}, u32[]{:S(2)}, u32[]{:S(2)}) async-start(bf16[64,16,256]{2,1,0:T(8,128)(2,1)} %bitcast.82), calls=%async_computation.3 | async-start | bytes 1048576 | tf_op jit(solution)/shard_map/all_to_all | solution.py:188
  130.0 6.6 %copy-start.9 = (f32[16,2,128]{2,1,0:T(2,128)S(1)}, f32[16,2,128]{2,1,0:T(2,128)}, u32[]{:S(2)}) copy-start(f32[16,2,128]{2,1,0:T(2,128)} %param.13) | copy-start | bytes 49156
  130.0 6.6 %copy-start.10 = (f32[16,2,128]{2,1,0:T(2,128)S(1)}, f32[16,2,128]{2,1,0:T(2,128)}, u32[]{:S(2)}) copy-start(f32[16,2,128]{2,1,0:T(2,128)} %param.14) | copy-start | bytes 49156
  130.0 6.6 %copy-start.11 = (f32[16,2,128]{2,1,0:T(2,128)S(1)}, f32[16,2,128]{2,1,0:T(2,128)}, u32[]{:S(2)}) copy-start(f32[16,2,128]{2,1,0:T(2,128)} %param.15) | copy-start | bytes 49156
  130.0 22.9 %all-to-all-start.2 = ((bf16[4,128,1280]{2,1,0:T(8,128)(2,1)}), bf16[4,128,1280]{2,1,0:T(8,128)(2,1)S(1)}, u32[]{:S(2)}, u32[]{:S(2)}) async-start(bf16[4,128,1280]{2,1,0:T(8,128)(2,1)} %bitcast.22), calls=%async_computation.2 | async-start | bytes 2621440 | tf_op jit(solution)/shard_map/all_to_all | solution.py:191

commit v2 on v1

v2 whole, which is shorter than its diff:
```python
import functools

import jax
import jax.numpy as jnp
from jax import lax
from jax.experimental import pallas as pl
from jax.experimental.pallas import tpu as pltpu
from jax.sharding import PartitionSpec as P

QUERY_HEADS = 32
KEY_VALUE_HEADS = 4
HEAD_WIDTH = 128
PREFIX_TOKENS = 1024
SLOT_COUNT = 512
STEP = 10

BETA_ONE = 0.9
BETA_TWO = 0.999
ADAM_EPS = 1e-08
LEARN_RATE = 0.01
MASKED = -1e30
GROUP = QUERY_HEADS // KEY_VALUE_HEADS
ALL_TOKENS = PREFIX_TOKENS + SLOT_COUNT
SCALE = HEAD_WIDTH ** (-0.5)
LOG2_SCALE = SCALE * 1.4426950408889634

PEERS = 4
OWN_ROWS = SLOT_COUNT // PEERS
PLANE = 16
PLANES = 4
SHARE = PREFIX_TOKENS // (PLANE * PLANES)
IN_PLANE = [[z * PLANE + r for r in range(PLANE)] for z in range(PLANES)]

HALVES = 2
HALF_HEADS = GROUP // HALVES
HALF = HALF_HEADS * HEAD_WIDTH
TOGETHER = 2
ROWS = 256
CHUNK = 512
BLOCKS = SLOT_COUNT // ROWS

bf16 = jnp.bfloat16
f32 = jnp.float32
VMEM = pl.BlockSpec(memory_space=pltpu.VMEM)
SMEM = pl.BlockSpec(memory_space=pltpu.SMEM)
PARAMS = pltpu.CompilerParams(vmem_limit_bytes=28 * 1024 * 1024)


def nn(a, b):
    return jnp.dot(a, b, preferred_element_type=f32)


def turned(a):
    return a.astype(f32).T


def part_start(place, peer, width):
    return pl.multiple_of(jnp.bitwise_xor(place, peer) * width, width)


def outgoing_kernel(place_ref, *refs):
    outs, held, sems = refs[4 : 4 + 2 * PEERS], refs[4 + 2 * PEERS : -1], refs[-1]
    copies = [pltpu.make_async_copy(refs[i], held[i], sems.at[i]) for i in range(4)]
    for copy in copies:
        copy.start()
    for copy in copies:
        copy.wait()
    q_ref, g_ref, k_ref, v_ref = held
    place = place_ref[0]
    for peer in range(PEERS):
        heads = part_start(place, peer, GROUP * HEAD_WIDTH)
        shared = pl.ds(part_start(place, peer, HEAD_WIDTH), HEAD_WIDTH)
        for half in range(HALVES):
            out = outs[half * PEERS + peer]
            own = pl.ds(pl.multiple_of(heads + half * HALF, HALF), HALF)
            out[:, :HALF] = q_ref[0, :, own]
            out[:, HALF : 2 * HALF] = g_ref[0, :, own]
        out = outs[peer]
        out[:, 2 * HALF : 2 * HALF + HEAD_WIDTH] = k_ref[0, :, shared]
        out[:, 2 * HALF + HEAD_WIDTH :] = v_ref[0, :, shared]


def outgoing(place, queries, out_grad, dialogue_keys, dialogue_values):
    first = jax.ShapeDtypeStruct((OWN_ROWS, 2 * HALF + 2 * HEAD_WIDTH), bf16)
    second = jax.ShapeDtypeStruct((OWN_ROWS, 2 * HALF), bf16)
    outs = pl.pallas_call(
        outgoing_kernel,
        in_specs=[SMEM] + [pl.BlockSpec(memory_space=pltpu.HBM)] * 4,
        out_specs=[VMEM] * (2 * PEERS),
        out_shape=[first] * PEERS + [second] * PEERS,
        scratch_shapes=[
            pltpu.VMEM(x.shape, bf16) for x in (queries, out_grad, dialogue_keys, dialogue_values)
        ]
        + [pltpu.SemaphoreType.DMA((4,))],
        compiler_params=pltpu.CompilerParams(vmem_limit_bytes=60 * 1024 * 1024),
        cost_estimate=pl.CostEstimate(flops=0, bytes_accessed=5 * 10**6, transcendentals=0),
    )(place, queries, out_grad, dialogue_keys, dialogue_values)
    return outs[:PEERS], outs[PEERS:]


def assemble_kernel(place_ref, *refs):
    first, second = refs[:PEERS], refs[PEERS : 2 * PEERS]
    q_ref, k_ref, v_ref = refs[2 * PEERS :]
    place = place_ref[0]
    for peer in range(PEERS):
        heads = part_start(place, peer, GROUP * HEAD_WIDTH)
        shared = pl.ds(part_start(place, peer, HEAD_WIDTH), HEAD_WIDTH)
        q_ref[0, :, pl.ds(heads, HALF)] = first[peer][...]
        q_ref[0, :, pl.ds(pl.multiple_of(heads + HALF, HALF), HALF)] = second[peer][:, :HALF]
        k_ref[0, :, shared] = second[peer][:, HALF : HALF + HEAD_WIDTH]
        v_ref[0, :, shared] = second[peer][:, HALF + HEAD_WIDTH :]


def assemble(place, first, second):
    narrow = jax.ShapeDtypeStruct((1, OWN_ROWS, KEY_VALUE_HEADS * HEAD_WIDTH), bf16)
    return pl.pallas_call(
        assemble_kernel,
        in_specs=[SMEM] + [VMEM] * (2 * PEERS),
        out_specs=[VMEM] * 3,
        out_shape=[jax.ShapeDtypeStruct((1, OWN_ROWS, QUERY_HEADS * HEAD_WIDTH), bf16), narrow, narrow],
        compiler_params=PARAMS,
        cost_estimate=pl.CostEstimate(flops=0, bytes_accessed=3 * 10**6, transcendentals=0),
    )(place, *first, *second)


class Unit:
    def __init__(self, slot, head, block):
        self.slot, self.head = slot, head
        self.first = block * ROWS
        self.rows = slice(self.first, self.first + ROWS)
        end = PREFIX_TOKENS + self.first + ROWS
        self.spans = [slice(s, min(s + CHUNK, end)) for s in range(0, end, CHUNK)]
        self.tops, self.top, self.total = [], None, None


def attention_kernel(last, length_ref, place_ref, *refs):
    tokens, shared = refs[:PEERS], refs[PEERS : 2 * PEERS]
    refs = refs[2 * PEERS :]
    prefix_refs, refs = refs[:PLANES], refs[PLANES:]
    if last:
        (dkeys_in, dvalues_in), refs = refs[:2], refs[2:]
    outs, refs = refs[:PEERS], refs[PEERS:]
    (dkeys_out, dvalues_out) = (None, None) if last else refs[:2]
    pgrad_ref = refs[0] if last else None
    refs = refs[1:] if last else refs[2:]
    keys, values, keys_t, values_t, dkeys, dvalues, exps, q_all, g_all, qgrad_all = refs
    if not last:
        dkeys, dvalues = dkeys_out, dvalues_out
    length, place = length_ref[0], place_ref[0]

    for k in range(PLANES):
        plane = slice(k * PLANE * SHARE, (k + 1) * PLANE * SHARE)
        keys[plane] = prefix_refs[k][:, :HEAD_WIDTH]
        values[plane] = prefix_refs[k][:, HEAD_WIDTH:]
    for peer in range(PEERS):
        rows = pl.ds(part_start(place, peer, OWN_ROWS), OWN_ROWS)
        there = pl.ds(pl.multiple_of(PREFIX_TOKENS + part_start(place, peer, OWN_ROWS), OWN_ROWS), OWN_ROWS)
        keys[there] = shared[peer][:, 2 * HALF : 2 * HALF + HEAD_WIDTH]
        values[there] = shared[peer][:, 2 * HALF + HEAD_WIDTH :]
        q_all[rows] = tokens[peer][:, :HALF]
        g_all[rows] = tokens[peer][:, HALF : 2 * HALF]
    for start in range(0, ALL_TOKENS, 256):
        span = slice(start, start + 256)
        keys_t[:, span] = turned(keys[span]).astype(bf16)
        values_t[:, span] = turned(values[span]).astype(bf16)
    dkeys[...] = jnp.zeros_like(dkeys)
    dvalues[...] = jnp.zeros_like(dvalues)

    def prepare(u):
        q = q_all[u.rows, u.head]
        row_index = u.first + lax.broadcasted_iota(jnp.int32, (ROWS, HEAD_WIDTH), 0)
        u.q = q
        u.g = jnp.where(row_index < length, g_all[u.rows, u.head], jnp.zeros((), bf16))
        u.q_t = turned(q).astype(bf16)
        u.g_wide = turned(u.g)
        u.g_t = u.g_wide.astype(bf16)

    def forward(u, i):
        span = u.spans[i]
        scores = nn(keys[span], u.q_t)
        masked = PREFIX_TOKENS + u.first
        if span.stop > masked:
            skip = max(span.start, masked) - span.start
            shape = (span.stop - span.start - skip, ROWS)
            key_pos = span.start + skip - PREFIX_TOKENS + lax.broadcasted_iota(jnp.int32, shape, 0)
            row_pos = u.first + lax.broadcasted_iota(jnp.int32, shape, 1)
            tail = jnp.where(key_pos <= row_pos, scores[skip:], MASKED)
            scores = jnp.concatenate([scores[:skip], tail], 0) if skip else tail
        top = jnp.max(scores, axis=0, keepdims=True)
        top = top if u.top is None else jnp.maximum(top, u.top)
        e = jnp.exp2((scores - top) * LOG2_SCALE)
        exps[u.slot, span] = e
        total = jnp.sum(e, axis=0, keepdims=True)
        u.total = total if u.top is None else u.total * jnp.exp2((u.top - top) * LOG2_SCALE) + total
        u.top = top
        u.tops.append(top)

    def end_forward(u):
        inverse = 1.0 / u.total
        u.factors = [jnp.exp2((top - u.top) * LOG2_SCALE) * inverse for top in u.tops]
        u.attended = jnp.zeros((HEAD_WIDTH, ROWS), f32)
        u.qgrad = jnp.zeros((HEAD_WIDTH, ROWS), f32)

    def attend(u, i):
        span = u.spans[i]
        half = (exps[u.slot, span] * u.factors[i]).astype(bf16)
        u.attended = u.attended + nn(values_t[:, span], half)
        dvalues[span] += nn(half, u.g)

    def end_attend(u):
        u.row_dot = jnp.sum(u.g_wide * u.attended.astype(bf16).astype(f32), axis=0, keepdims=True)

    def backward(u, i):
        span = u.spans[i]
        weight_grad = nn(values[span], u.g_t)
        score_grad = (exps[u.slot, span] * u.factors[i] * (weight_grad - u.row_dot)).astype(bf16)
        u.qgrad = u.qgrad + nn(keys_t[:, span], score_grad)
        dkeys[span] += nn(score_grad, u.q)

    def end_backward(u):
        qgrad_all[u.rows, u.head] = (u.qgrad * SCALE).T.astype(bf16)

    def some_heads(step, carry):
        units = []
        for h in range(TOGETHER):
            start = pl.multiple_of((step * TOGETHER + h) * HEAD_WIDTH, HEAD_WIDTH)
            for block in range(BLOCKS):
                units.append(Unit(len(units), pl.ds(start, HEAD_WIDTH), block))
        for u in units:
            prepare(u)
        stages = ((forward, end_forward), (attend, end_attend), (backward, end_backward))
        for t in range(len(units) + len(stages) - 1):
            live = [(units[t - s], *stages[s]) for s in range(len(stages)) if 0 <= t - s < len(units)]
            for i in range(max(len(u.spans) for u, _, _ in live)):
                for u, work, _ in live:
                    if i < len(u.spans):
                        work(u, i)
            for u, _, end in live:
                end(u)
        return carry

    lax.fori_loop(0, HALF_HEADS // TOGETHER, some_heads, 0)

    for peer in range(PEERS):
        rows = pl.ds(part_start(place, peer, OWN_ROWS), OWN_ROWS)
        outs[peer][:, :HALF] = qgrad_all[rows]
        if last:
            there = pl.ds(pl.multiple_of(PREFIX_TOKENS + part_start(place, peer, OWN_ROWS), OWN_ROWS), OWN_ROWS)
            outs[peer][:, HALF : HALF + HEAD_WIDTH] = ((dkeys[there] + dkeys_in[there]) * SCALE).astype(bf16)
            outs[peer][:, HALF + HEAD_WIDTH :] = (dvalues[there] + dvalues_in[there]).astype(bf16)
    if last:
        for k in range(PLANE * PLANES):
            rows = slice(k * SHARE, (k + 1) * SHARE)
            there = jnp.bitwise_xor(place_ref[1], (k // PLANES % 4) * 4 + k // PLANE), k % PLANES
            pgrad_ref[there[0], there[1], :, :HEAD_WIDTH] = ((dkeys[rows] + dkeys_in[rows]) * SCALE).astype(bf16)
            pgrad_ref[there[0], there[1], :, HEAD_WIDTH:] = (dvalues[rows] + dvalues_in[rows]).astype(bf16)


def attention(length, place, tokens, shared, prefix, sums=None):
    last = sums is not None
    out = jax.ShapeDtypeStruct((OWN_ROWS, HALF + (2 * HEAD_WIDTH if last else 0)), bf16)
    running = jax.ShapeDtypeStruct((ALL_TOKENS, HEAD_WIDTH), f32)
    outs = [out] * PEERS
    outs += [jax.ShapeDtypeStruct((PLANE, PLANES, SHARE, 2 * HEAD_WIDTH), bf16)] if last else [running] * 2
    operands = (*tokens, *shared, *prefix, *(sums or ()))
    half = pltpu.VMEM((ALL_TOKENS, HEAD_WIDTH), bf16)
    half_t = pltpu.VMEM((HEAD_WIDTH, ALL_TOKENS), bf16)
    wide = pltpu.VMEM((ALL_TOKENS, HEAD_WIDTH), f32)
    every = pltpu.VMEM((SLOT_COUNT, HALF), bf16)
    small = pltpu.VMEM((8, HEAD_WIDTH), f32)
    total = wide if last else small
    return pl.pallas_call(
        functools.partial(attention_kernel, last),
        in_specs=[SMEM] * 2 + [VMEM] * len(operands),
        out_specs=[VMEM] * len(outs),
        out_shape=outs,
        scratch_shapes=[
            half, half, half_t, half_t, total, total,
            pltpu.VMEM((TOGETHER * BLOCKS, ALL_TOKENS, ROWS), f32),
            every, every, every,
        ],
        compiler_params=PARAMS,
        cost_estimate=pl.CostEstimate(flops=5 * 10**9, bytes_accessed=5 * 10**6, transcendentals=3 * 10**6),
    )(length, place, *operands)


def shards(
    queries,
    dialogue_keys,
    dialogue_values,
    out_grad,
    lengths,
    cartridge,
    first_moment,
    second_moment,
):
    place = jnp.stack([lax.axis_index("tensor"), lax.axis_index("dp") % PLANE])

    def exchange(parts):
        return [
            lax.ppermute(part, "tensor", [(i, i ^ peer) for i in range(PEERS)]) if peer else part
            for peer, part in enumerate(parts)
        ]

    def across(parts, stride=PLANE):
        size = PLANE * PLANES
        return [
            lax.ppermute(part, "dp", [(i, i ^ (k * stride)) for i in range(size)]) if k else part
            for k, part in enumerate(parts)
        ]

    own_prefix = cartridge.astype(bf16).reshape(SHARE, 2 * HEAD_WIDTH)
    column = across([own_prefix] * 4)
    first, second = outgoing(place, queries, out_grad, dialogue_keys, dialogue_values)
    column, own_part = lax.optimization_barrier((column, first[0]))
    first = [own_part, *first[1:]]
    column = jnp.concatenate(column)
    plane = jnp.concatenate(across([column] * 4, 4))
    prefix = across([plane] * 4, 1)
    first = exchange(first)
    first, second = lax.optimization_barrier((first, second))
    second = exchange(second)

    *first_grad, key_sum, value_sum = attention(lengths, place, first, first, prefix)
    first_back = exchange(first_grad)
    *second_grad, prefix_part = attention(lengths, place, second, first, prefix, (key_sum, value_sum))

    arrived = lax.all_to_all(prefix_part, "dp", 0, 0, axis_index_groups=IN_PLANE)
    second_back = exchange(second_grad)
    plane_sum = jnp.sum(arrived.astype(f32), 0).astype(bf16)
    arrived = across([plane_sum[k] for k in range(PLANES)])
    prefix_grad = sum(part.astype(f32) for part in arrived).reshape(cartridge.shape)
    q_grad, key_grad, value_grad = assemble(place, first_back, second_back)

    new_m = BETA_ONE * first_moment + (1.0 - BETA_ONE) * prefix_grad
    new_v = BETA_TWO * second_moment + (1.0 - BETA_TWO) * prefix_grad * prefix_grad
    update = new_m / (1.0 - BETA_ONE**STEP) / (jnp.sqrt(new_v / (1.0 - BETA_TWO**STEP)) + ADAM_EPS)
    new_cartridge = cartridge - LEARN_RATE * update
    return (q_grad, key_grad, value_grad, new_cartridge, new_m, new_v)


def solution(mesh):
    tokens = P("dp", "tensor", None)
    trained = P("dp", None, "tensor")
    return jax.shard_map(
        shards,
        mesh=mesh,
        in_specs=(tokens, tokens, tokens, tokens, P("dp"), trained, trained, trained),
        out_specs=(tokens, tokens, tokens, trained, trained, trained),
        check_vma=False,
    )
```

time: 156 us -> 95.1 us (0.61)
  waiting for transfers between devices: 72 us -> 17.8 us
  starting transfers between devices: 34.9 us -> 40.5 us
  other arithmetic: 7.05 us -> 2.07 us
  local copies, waits for them, and re-layouts: 6.55 us -> 1.72 us
  Pallas kernels: 33.6 us -> 31.2 us
    all_to_all x4 -> x1, waiting for transfers between devices: 72 us -> 7.87 us  [shards(): lax.all_to_all(prefix_part, 'dp', 0, 0, axis_index_groups=IN_PLANE)]
    ppermute x0 -> x24, starting transfers between devices: none -> 34.3 us  [the longest x12 22.5 us: across(): lax.ppermute(part, 'dp', [(i, i ^ k * stride) for i in range(size)])]
    all_to_all x4 -> x1, starting transfers between devices: 34.9 us -> 6.2 us  [shards(): lax.all_to_all(prefix_part, 'dp', 0, 0, axis_index_groups=IN_PLANE)]
    ppermute x0 -> x24, waiting for transfers between devices: none -> 9.96 us  [the longest x12 6.02 us: across(): lax.ppermute(part, 'dp', [(i, i ^ k * stride) for i in range(size)])]
    unnamed x25 -> x20, local copies, waits for them, and re-layouts: 5.32 us -> 1.7 us
    pallas_call x1 -> x4, Pallas kernels: 33.6 us -> 31.2 us  [the longest x2 25.6 us: attention(): pl.pallas_call(functools.partial(attention_kernel, last), in_specs=[SMEM]...]
    broadcast_in_dim x3 -> x0, other arithmetic: 2.39 us -> none  [the longest x1 1.05 us: shards(): jnp.concatenate([returned[t, :, :head_columns] for t in range(tensor_size...]
  transfers between devices with their start and end apart: 4 -> 25, of which waited for: 4 -> 8; matrix products, arithmetic and copies ran while one was open for 3% -> 1% of each run, Pallas kernels for 0% -> 19%
where the time goes in v2:
time: 95.1 us; the launch traced here: 94.8 us
  starting transfers between devices  40.5 us (43%)
  Pallas kernels  31.2 us (33%)
  waiting for transfers between devices  17.8 us (19%)
  other arithmetic  2.07 us (2%)
  local copies, waits for them, and re-layouts  1.72 us (2%)
  between operations  1.46 us (2%)
    pallas_call x2, Pallas kernels, attention(): pl.pallas_call(functools.partial(attention_kernel, last), in_specs=[SMEM]...  25.6 us
    ppermute x12, starting transfers between devices, across(): lax.ppermute(part, 'dp', [(i, i ^ k * stride) for i in range(size)])  22.5 us
    ppermute x12, starting transfers between devices, exchange(): lax.ppermute(part, 'tensor', [(i, i ^ peer) for i in range(PEERS)])  11.8 us
    all_to_all x1, waiting for transfers between devices, shards(): lax.all_to_all(prefix_part, 'dp', 0, 0, axis_index_groups=IN_PLANE)  7.87 us
    all_to_all x1, starting transfers between devices, shards(): lax.all_to_all(prefix_part, 'dp', 0, 0, axis_index_groups=IN_PLANE)  6.2 us
    ppermute x12, waiting for transfers between devices, across(): lax.ppermute(part, 'dp', [(i, i ^ k * stride) for i in range(size)])  6.02 us
    ppermute x12, waiting for transfers between devices, exchange(): lax.ppermute(part, 'tensor', [(i, i ^ peer) for i in range(PEERS)])  3.93 us
    pallas_call x1, Pallas kernels, outgoing(): pl.pallas_call(outgoing_kernel, in_specs=[SMEM] + [pl.BlockSpec(memory_sp...  3.85 us
  transfers between devices with their start and end apart: 25, of which 8 were waited for; matrix products, arithmetic and copies ran while one was open for 1% of the time, Pallas kernels for 19%

profile of v2, /device:TPU:1, one launch (start us, length us, event | category | flops | bytes accessed | tf_op | source)
XLA Modules:
  0.0 94.8 jit_solution(2399360002402839223)
XLA Ops:
  0.6 0.7 convert_element_type.20
  1.4 3.9 %collective-permute-start = (bf16[16,256]{1,0:T(8,128)(2,1)S(1)}, bf16[16,256]{1,0:T(8,128)(2,1)S(1)}, u32[]{:S(2)}, u32[]{:S(2)}) collective-permute-start(bf16[16,256]{1,0:T(8,128)(2,1)S(1)} %bitcast.17), channel_id=1, source_target_pairs={{0,64},{4,68},{8,72},{12,76},{16,80},{20,84},{24,88},{28,92},{32,9... | collective-permute-start | bytes 24584 | tf_op jit(solution)/shard_map/ppermute | solution.py:308
  5.3 5.1 %collective-permute-start.1 = (bf16[16,256]{1,0:T(8,128)(2,1)S(1)}, bf16[16,256]{1,0:T(8,128)(2,1)S(1)}, u32[]{:S(2)}, u32[]{:S(2)}) collective-permute-start(bf16[16,256]{1,0:T(8,128)(2,1)S(1)} %bitcast.18), channel_id=1, source_target_pairs={{0,128},{4,132},{8,136},{12,140},{16,144},{20,148},{24,152},{28,15... | collective-permute-start | bytes 24584 | tf_op jit(solution)/shard_map/ppermute | solution.py:308
  11.0 3.9 %shard_map.127 = (bf16[128,1280]{1,0:T(8,128)(2,1)}, bf16[128,1280]{1,0:T(8,128)(2,1)}, bf16[128,1280]{1,0:T(8,128)(2,1)}, bf16[128,1280]{1,0:T(8,128)(2,1)}, bf...) custom-call(s32[2]{0:T(128)} %pad_add_fusion.place_ref, ...), custom_call_target="tpu_custom_call" | custom-call | bytes 5000000 | tf_op jit(solution)/shard_map/pallas_call | solution.py:86
  15.0 1.4 %collective-permute-start.6 = (bf16[64,256]{1,0:T(8,128)(2,1)S(1)}, bf16[64,256]{1,0:T(8,128)(2,1)S(1)}, u32[]{:S(2)}, u32[]{:S(2)}) collective-permute-start(bf16[64,256]{1,0:T(8,128)(2,1)S(1)} %get-tuple-element.82), channel_id=1, source_target_pairs={{0,16},{4,20},{8,24},{12,28},{16,0},{20,4},{24,8},{28,12},{32,48},... | collective-permute-start | bytes 98312 | tf_op jit(solution)/shard_map/ppermute | solution.py:308
  16.4 2.7 %collective-permute-start.3 = (bf16[128,1280]{1,0:T(8,128)(2,1)}, bf16[128,1280]{1,0:T(8,128)(2,1)S(1)}, u32[]{:S(2)}, u32[]{:S(2)}) collective-permute-start(bf16[128,1280]{1,0:T(8,128)(2,1)} %get-tuple-element.43), channel_id=1, source_target_pairs={{0,1},{1,0},{2,3},{3,2},{4,5},{5,4},{6,7},{7,6},{8,9},{9,8},{10,11... | collective-permute-start | bytes 983048 | tf_op jit(solution)/shard_map/ppermute | solution.py:301
  19.1 0.7 collective-permute-start.4
  19.8 0.9 collective-permute-start.5
  20.7 2.6 %collective-permute-start.7 = (bf16[64,256]{1,0:T(8,128)(2,1)S(1)}, bf16[64,256]{1,0:T(8,128)(2,1)S(1)}, u32[]{:S(2)}, u32[]{:S(2)}) collective-permute-start(bf16[64,256]{1,0:T(8,128)(2,1)S(1)} %get-tuple-element.82), channel_id=1, source_target_pairs={{0,32},{4,36},{8,40},{12,44},{16,48},{20,52},{24,56},{28,60},{32,0... | collective-permute-start | bytes 98312 | tf_op jit(solution)/shard_map/ppermute | solution.py:308
  23.3 1.6 %collective-permute-done.7 = bf16[64,256]{1,0:T(8,128)(2,1)S(1)} collective-permute-done((bf16[64,256]{1,0:T(8,128)(2,1)S(1)}, bf16[64,256]{1,0:T(8,128)(2,1)S(1)}, u32[]{:S(2)}, u32[]{:S(2)}) %collective-permute-start.7) | collective-permute-done | bytes 32800 | tf_op jit(solution)/shard_map/ppermute | solution.py:308
  25.0 2.3 %collective-permute-done.8 = bf16[64,256]{1,0:T(8,128)(2,1)S(1)} collective-permute-done((bf16[64,256]{1,0:T(8,128)(2,1)S(1)}, bf16[64,256]{1,0:T(8,128)(2,1)S(1)}, u32[]{:S(2)}, u32[]{:S(2)}) %collective-permute-start.8) | collective-permute-done | bytes 32800 | tf_op jit(solution)/shard_map/ppermute | solution.py:308
  27.3 1.2 %collective-permute-start.9 = (bf16[256,256]{1,0:T(8,128)(2,1)S(1)}, bf16[256,256]{1,0:T(8,128)(2,1)S(1)}, u32[]{:S(2)}, u32[]{:S(2)}) collective-permute-start(bf16[256,256]{1,0:T(8,128)(2,1)S(1)} %constant_dynamic-update-slice_fusion.4.refs_8_), channel_id=1, source_target_pairs={{0,4},{4,0},{8,12},{12,8},{16,20},{20,16},{24,28},{28,24},{32,36},... | collective-permute-start | bytes 393224 | tf_op jit(solution)/shard_map/ppermute | solution.py:308
  28.5 2.5 %collective-permute-start.10 = (bf16[256,256]{1,0:T(8,128)(2,1)S(1)}, bf16[256,256]{1,0:T(8,128)(2,1)S(1)}, u32[]{:S(2)}, u32[]{:S(2)}) collective-permute-start(bf16[256,256]{1,0:T(8,128)(2,1)S(1)} %constant_dynamic-update-slice_fusion.4.refs_8_), channel_id=1, source_target_pairs={{0,8},{4,12},{8,0},{12,4},{16,24},{20,28},{24,16},{28,20},{32,40},... | collective-permute-start | bytes 393224 | tf_op jit(solution)/shard_map/ppermute | solution.py:308
  31.8 3.9 %collective-permute-done.5.refs_3_.refs_7_ = bf16[128,1280]{1,0:T(8,128)(2,1)S(1)} collective-permute-done((bf16[128,1280]{1,0:T(8,128)(2,1)}, bf16[128,1280]{1,0:T(8,128)(2,1)S(1)}, u32[]{:S(2)}, u32[]{:S(2)}) %collective-permute-start.5) | collective-permute-done | bytes 327712 | tf_op jit(solution)/shard_map/ppermute | solution.py:301
  36.0 0.7 collective-permute-start.16
  36.8 1.1 %collective-permute-start.17 = (bf16[128,1024]{1,0:T(8,128)(2,1)S(1)}, bf16[128,1024]{1,0:T(8,128)(2,1)S(1)}, u32[]{:S(2)}, u32[]{:S(2)}) collective-permute-start(bf16[128,1024]{1,0:T(8,128)(2,1)S(1)} %copy-done.6), channel_id=1, source_target_pairs={{0,3},{1,2},{2,1},{3,0},{4,7},{5,6},{6,5},{7,4},{8,11},{9,10},{10,... | collective-permute-start | bytes 786440 | tf_op jit(solution)/shard_map/ppermute | solution.py:301
  38.2 1.0 %copy-done.1 = bf16[128,1280]{1,0:T(8,128)(2,1)S(1)} copy-done((bf16[128,1280]{1,0:T(8,128)(2,1)S(1)}, bf16[128,1280]{1,0:T(8,128)(2,1)}, u32[]{:S(2)}) %copy-start.1) | copy-done | bytes 327704
  39.1 12.3 %shard_map.128 = (bf16[128,512]{1,0:T(8,128)(2,1)S(1)}, bf16[128,512]{1,0:T(8,128)(2,1)S(1)}, bf16[128,512]{1,0:T(8,128)(2,1)S(1)}, bf16[128,512]{1,0:T(8,128)(2...) custom-call(s32[1]{0:T(128)S(6)} %copy.26.length_ref, s32[2]{0:T(128)S(1)} %copy-done, ...), custom_call_target="tpu_custom_call" | custom-call | flops 5000000000 | bytes 5000000 | tf_op jit(solution)/shard_map/pallas_call | solution.py:272
  51.5 13.3 %shard_map.129 = (bf16[128,768]{1,0:T(8,128)(2,1)S(1)}, bf16[128,768]{1,0:T(8,128)(2,1)S(1)}, bf16[128,768]{1,0:T(8,128)(2,1)S(1)}, bf16[128,768]{1,0:T(8,128)(2,1)S(1)}, bf16[16,4,16,256]{3,2,1,0:T(8,128)(2,1)}) custom-call(s32[1]{0:T(128)S(6)} %copy.26.length_ref, s32[2]{0:T(128)S(1)} %copy-done, bf16[128,1024]{1,0:T(8,128)(2,1)S(1)} %copy-done.2, ...), custom_call_target="tpu_custom_call" | custom-call | flops 5000000000 | bytes 5000000 | tf_op jit(solution)/shard_map/pallas_call | solution.py:272
  64.8 6.2 %all-to-all-start = ((bf16[16,4,16,256]{3,2,1,0:T(8,128)(2,1)}), bf16[16,4,16,256]{3,2,1,0:T(8,128)(2,1)S(1)}, u32[]{:S(2)}, u32[]{:S(2)}) async-start(bf16[16,4,16,256]{3,2,1,0:T(8,128)(2,1)} %get-tuple-element.75), calls=%async_computation | async-start | bytes 1048576 | tf_op jit(solution)/shard_map/all_to_all | solution.py:328
  71.6 0.7 collective-permute-start.13
  72.4 1.1 %collective-permute-start.14 = (bf16[128,512]{1,0:T(8,128)(2,1)S(1)}, bf16[128,512]{1,0:T(8,128)(2,1)S(1)}, u32[]{:S(2)}, u32[]{:S(2)}) collective-permute-start(bf16[128,512]{1,0:T(8,128)(2,1)S(1)} %get-tuple-element.61), channel_id=1, source_target_pairs={{0,3},{1,2},{2,1},{3,0},{4,7},{5,6},{6,5},{7,4},{8,11},{9,10},{10,... | collective-permute-start | bytes 393224 | tf_op jit(solution)/shard_map/ppermute | solution.py:301
  73.5 0.7 collective-permute-start.19
  74.2 7.9 %all-to-all-done = bf16[16,4,16,256]{3,2,1,0:T(8,128)(2,1)S(1)} async-done(((bf16[16,4,16,256]{3,2,1,0:T(8,128)(2,1)}), bf16[16,4,16,256]{3,2,1,0:T(8,128)(2,1)S(1)}, u32[]{:S(2)}, u32[]{:S(2)}) %all-to-all-start) | async-done | bytes 524320 | tf_op jit(solution)/shard_map/all_to_all | solution.py:328
  82.2 2.1 %collective-permute-start.20 = (bf16[128,768]{1,0:T(8,128)(2,1)S(1)}, bf16[128,768]{1,0:T(8,128)(2,1)S(1)}, u32[]{:S(2)}, u32[]{:S(2)}) collective-permute-start(bf16[128,768]{1,0:T(8,128)(2,1)S(1)} %get-tuple-element.71), channel_id=1, source_target_pairs={{0,3},{1,2},{2,1},{3,0},{4,7},{5,6},{6,5},{7,4},{8,11},{9,10},{10,... | collective-permute-start | bytes 589832 | tf_op jit(solution)/shard_map/ppermute | solution.py:301
  84.3 2.6 %collective-permute-start.23 = (bf16[16,256]{1,0:T(8,128)(2,1)S(1)}, bf16[16,256]{1,0:T(8,128)(2,1)S(1)}, u32[]{:S(2)}, u32[]{:S(2)}) collective-permute-start(bf16[16,256]{1,0:T(8,128)(2,1)S(1)} %get-tuple-element.80), channel_id=1, source_target_pairs={{0,192},{4,196},{8,200},{12,204},{16,208},{20,212},{24,216},{28,22... | collective-permute-start | bytes 24584 | tf_op jit(solution)/shard_map/ppermute | solution.py:308
  86.9 1.9 %collective-permute-start.22 = (bf16[16,256]{1,0:T(8,128)(2,1)S(1)}, bf16[16,256]{1,0:T(8,128)(2,1)S(1)}, u32[]{:S(2)}, u32[]{:S(2)}) collective-permute-start(bf16[16,256]{1,0:T(8,128)(2,1)S(1)} %get-tuple-element.81), channel_id=1, source_target_pairs={{0,128},{4,132},{8,136},{12,140},{16,144},{20,148},{24,152},{28,15... | collective-permute-start | bytes 24584 | tf_op jit(solution)/shard_map/ppermute | solution.py:308
  88.8 1.2 %collective-permute-start.21 = (bf16[16,256]{1,0:T(8,128)(2,1)S(1)}, bf16[16,256]{1,0:T(8,128)(2,1)S(1)}, u32[]{:S(2)}, u32[]{:S(2)}) collective-permute-start(bf16[16,256]{1,0:T(8,128)(2,1)S(1)} %get-tuple-element.79), channel_id=1, source_target_pairs={{0,64},{4,68},{8,72},{12,76},{16,80},{20,84},{24,88},{28,92},{32,9... | collective-permute-start | bytes 24584 | tf_op jit(solution)/shard_map/ppermute | solution.py:308
  90.0 1.7 %shard_map.130 = (bf16[1,128,4096]{2,1,0:T(8,128)(2,1)}, bf16[1,128,512]{2,1,0:T(8,128)(2,1)}, bf16[1,128,512]{2,1,0:T(8,128)(2,1)}) custom-call(s32[2]{0:T(128)S(1)} %copy-done, bf16[128,512]{1,0:T(8,128)(2,1)S(1)} %get-tuple-element.58.refs_0_, bf16[128,512]{1,0:T(8,128)(2,1)S(1)} %collective-permute-done.12.refs_1_, ...), custom_call_target="tpu_custom_call" | custom-call | bytes 3000000 | tf_op jit(solution)/shard_map/pallas_call | solution.py:116
  91.8 1.5 %collective-permute-done.22 = bf16[16,256]{1,0:T(8,128)(2,1)S(1)} collective-permute-done((bf16[16,256]{1,0:T(8,128)(2,1)S(1)}, bf16[16,256]{1,0:T(8,128)(2,1)S(1)}, u32[]{:S(2)}, u32[]{:S(2)}) %collective-permute-start.22) | collective-permute-done | bytes 8224 | tf_op jit(solution)/shard_map/ppermute | solution.py:308
  93.4 0.7 copy-done.3
  94.1 0.7 multiply_subtract_fusion
  (51 shorter events, 2.5 us)
Async XLA Ops:
  1.4 13.5 %collective-permute-start = (bf16[16,256]{1,0:T(8,128)(2,1)S(1)}, bf16[16,256]{1,0:T(8,128)(2,1)S(1)}, u32[]{:S(2)}, u32[]{:S(2)}) collective-permute-start(bf16[16,256]{1,0:T(8,128)(2,1)S(1)} %bitcast.17), channel_id=1, source_target_pairs={{0,64},{4,68},{8,72},{12,76},{16,80},{20,84},{24,88},{28,92},{32,9... | collective-permute-start | bytes 24584 | tf_op jit(solution)/shard_map/ppermute | solution.py:308
  5.3 9.6 %collective-permute-start.1 = (bf16[16,256]{1,0:T(8,128)(2,1)S(1)}, bf16[16,256]{1,0:T(8,128)(2,1)S(1)}, u32[]{:S(2)}, u32[]{:S(2)}) collective-permute-start(bf16[16,256]{1,0:T(8,128)(2,1)S(1)} %bitcast.18), channel_id=1, source_target_pairs={{0,128},{4,132},{8,136},{12,140},{16,144},{20,148},{24,152},{28,15... | collective-permute-start | bytes 24584 | tf_op jit(solution)/shard_map/ppermute | solution.py:308
  10.4 4.6 %collective-permute-start.2 = (bf16[16,256]{1,0:T(8,128)(2,1)S(1)}, bf16[16,256]{1,0:T(8,128)(2,1)S(1)}, u32[]{:S(2)}, u32[]{:S(2)}) collective-permute-start(bf16[16,256]{1,0:T(8,128)(2,1)S(1)} %bitcast.19), channel_id=1, source_target_pairs={{0,192},{4,196},{8,200},{12,204},{16,208},{20,212},{24,216},{28,22... | collective-permute-start | bytes 24584 | tf_op jit(solution)/shard_map/ppermute | solution.py:308
  14.8 21.9 %copy-start.6 = (bf16[128,1024]{1,0:T(8,128)(2,1)S(1)}, bf16[128,1024]{1,0:T(8,128)(2,1)}, u32[]{:S(2)}) copy-start(bf16[128,1024]{1,0:T(8,128)(2,1)} %get-tuple-element.65) | copy-start | bytes 786436
  15.0 8.3 %collective-permute-start.6 = (bf16[64,256]{1,0:T(8,128)(2,1)S(1)}, bf16[64,256]{1,0:T(8,128)(2,1)S(1)}, u32[]{:S(2)}, u32[]{:S(2)}) collective-permute-start(bf16[64,256]{1,0:T(8,128)(2,1)S(1)} %get-tuple-element.82), channel_id=1, source_target_pairs={{0,16},{4,20},{8,24},{12,28},{16,0},{20,4},{24,8},{28,12},{32,48},... | collective-permute-start | bytes 98312 | tf_op jit(solution)/shard_map/ppermute | solution.py:308
  16.4 14.6 %collective-permute-start.3 = (bf16[128,1280]{1,0:T(8,128)(2,1)}, bf16[128,1280]{1,0:T(8,128)(2,1)S(1)}, u32[]{:S(2)}, u32[]{:S(2)}) collective-permute-start(bf16[128,1280]{1,0:T(8,128)(2,1)} %get-tuple-element.43), channel_id=1, source_target_pairs={{0,1},{1,0},{2,3},{3,2},{4,5},{5,4},{6,7},{7,6},{8,9},{9,8},{10,11... | collective-permute-start | bytes 983048 | tf_op jit(solution)/shard_map/ppermute | solution.py:301
  19.1 12.8 %collective-permute-start.4 = (bf16[128,1280]{1,0:T(8,128)(2,1)}, bf16[128,1280]{1,0:T(8,128)(2,1)S(1)}, u32[]{:S(2)}, u32[]{:S(2)}) collective-permute-start(bf16[128,1280]{1,0:T(8,128)(2,1)} %get-tuple-element.44), channel_id=1, source_target_pairs={{0,2},{1,3},{2,0},{3,1},{4,6},{5,7},{6,4},{7,5},{8,10},{9,11},{10,... | collective-permute-start | bytes 983048 | tf_op jit(solution)/shard_map/ppermute | solution.py:301
  19.8 15.9 %collective-permute-start.5 = (bf16[128,1280]{1,0:T(8,128)(2,1)}, bf16[128,1280]{1,0:T(8,128)(2,1)S(1)}, u32[]{:S(2)}, u32[]{:S(2)}) collective-permute-start(bf16[128,1280]{1,0:T(8,128)(2,1)} %get-tuple-element.45), channel_id=1, source_target_pairs={{0,3},{1,2},{2,1},{3,0},{4,7},{5,6},{6,5},{7,4},{8,11},{9,10},{10,... | collective-permute-start | bytes 983048 | tf_op jit(solution)/shard_map/ppermute | solution.py:301
  20.7 4.3 %collective-permute-start.7 = (bf16[64,256]{1,0:T(8,128)(2,1)S(1)}, bf16[64,256]{1,0:T(8,128)(2,1)S(1)}, u32[]{:S(2)}, u32[]{:S(2)}) collective-permute-start(bf16[64,256]{1,0:T(8,128)(2,1)S(1)} %get-tuple-element.82), channel_id=1, source_target_pairs={{0,32},{4,36},{8,40},{12,44},{16,48},{20,52},{24,56},{28,60},{32,0... | collective-permute-start | bytes 98312 | tf_op jit(solution)/shard_map/ppermute | solution.py:308
  23.3 4.0 %collective-permute-start.8 = (bf16[64,256]{1,0:T(8,128)(2,1)S(1)}, bf16[64,256]{1,0:T(8,128)(2,1)S(1)}, u32[]{:S(2)}, u32[]{:S(2)}) collective-permute-start(bf16[64,256]{1,0:T(8,128)(2,1)S(1)} %get-tuple-element.82), channel_id=1, source_target_pairs={{0,48},{4,52},{8,56},{12,60},{16,32},{20,36},{24,40},{28,44},{32,1... | collective-permute-start | bytes 98312 | tf_op jit(solution)/shard_map/ppermute | solution.py:308
  27.3 9.5 %collective-permute-start.9 = (bf16[256,256]{1,0:T(8,128)(2,1)S(1)}, bf16[256,256]{1,0:T(8,128)(2,1)S(1)}, u32[]{:S(2)}, u32[]{:S(2)}) collective-permute-start(bf16[256,256]{1,0:T(8,128)(2,1)S(1)} %constant_dynamic-update-slice_fusion.4.refs_8_), channel_id=1, source_target_pairs={{0,4},{4,0},{8,12},{12,8},{16,20},{20,16},{24,28},{28,24},{32,36},... | collective-permute-start | bytes 393224 | tf_op jit(solution)/shard_map/ppermute | solution.py:308
  28.5 9.4 %collective-permute-start.10 = (bf16[256,256]{1,0:T(8,128)(2,1)S(1)}, bf16[256,256]{1,0:T(8,128)(2,1)S(1)}, u32[]{:S(2)}, u32[]{:S(2)}) collective-permute-start(bf16[256,256]{1,0:T(8,128)(2,1)S(1)} %constant_dynamic-update-slice_fusion.4.refs_8_), channel_id=1, source_target_pairs={{0,8},{4,12},{8,0},{12,4},{16,24},{20,28},{24,16},{28,20},{32,40},... | collective-permute-start | bytes 393224 | tf_op jit(solution)/shard_map/ppermute | solution.py:308
  31.0 7.2 %collective-permute-start.11 = (bf16[256,256]{1,0:T(8,128)(2,1)S(1)}, bf16[256,256]{1,0:T(8,128)(2,1)S(1)}, u32[]{:S(2)}, u32[]{:S(2)}) collective-permute-start(bf16[256,256]{1,0:T(8,128)(2,1)S(1)} %constant_dynamic-update-slice_fusion.4.refs_8_), channel_id=1, source_target_pairs={{0,12},{4,8},{8,4},{12,0},{16,28},{20,24},{24,20},{28,16},{32,44},... | collective-permute-start | bytes 393224 | tf_op jit(solution)/shard_map/ppermute | solution.py:308
  35.7 2.4 %copy-start = (s32[2]{0:T(128)S(1)}, s32[2]{0:T(128)}, u32[]{:S(2)}) copy-start(s32[2]{0:T(128)} %pad_add_fusion.place_ref) | copy-start | bytes 28
  35.7 15.8 %collective-permute-start.15 = (bf16[128,1024]{1,0:T(8,128)(2,1)}, bf16[128,1024]{1,0:T(8,128)(2,1)S(1)}, u32[]{:S(2)}, u32[]{:S(2)}) collective-permute-start(bf16[128,1024]{1,0:T(8,128)(2,1)} %get-tuple-element.63), channel_id=1, source_target_pairs={{0,1},{1,0},{2,3},{3,2},{4,5},{5,4},{6,7},{7,6},{8,9},{9,8},{10,11... | collective-permute-start | bytes 786440 | tf_op jit(solution)/shard_map/ppermute | solution.py:301
  36.0 15.5 %collective-permute-start.16 = (bf16[128,1024]{1,0:T(8,128)(2,1)}, bf16[128,1024]{1,0:T(8,128)(2,1)S(1)}, u32[]{:S(2)}, u32[]{:S(2)}) collective-permute-start(bf16[128,1024]{1,0:T(8,128)(2,1)} %get-tuple-element.64), channel_id=1, source_target_pairs={{0,2},{1,3},{2,0},{3,1},{4,6},{5,7},{6,4},{7,5},{8,10},{9,11},{10,... | collective-permute-start | bytes 786440 | tf_op jit(solution)/shard_map/ppermute | solution.py:301
  36.8 14.7 %collective-permute-start.17 = (bf16[128,1024]{1,0:T(8,128)(2,1)S(1)}, bf16[128,1024]{1,0:T(8,128)(2,1)S(1)}, u32[]{:S(2)}, u32[]{:S(2)}) collective-permute-start(bf16[128,1024]{1,0:T(8,128)(2,1)S(1)} %copy-done.6), channel_id=1, source_target_pairs={{0,3},{1,2},{2,1},{3,0},{4,7},{5,6},{6,5},{7,4},{8,11},{9,10},{10,... | collective-permute-start | bytes 786440 | tf_op jit(solution)/shard_map/ppermute | solution.py:301
  38.2 1.0 %copy-start.1 = (bf16[128,1280]{1,0:T(8,128)(2,1)S(1)}, bf16[128,1280]{1,0:T(8,128)(2,1)}, u32[]{:S(2)}) copy-start(bf16[128,1280]{1,0:T(8,128)(2,1)} %get-tuple-element.50.refs_0_.refs_4_) | copy-start | bytes 983044
  39.1 12.4 %copy-start.2 = (bf16[128,1024]{1,0:T(8,128)(2,1)S(1)}, bf16[128,1024]{1,0:T(8,128)(2,1)}, u32[]{:S(2)}) copy-start(bf16[128,1024]{1,0:T(8,128)(2,1)} %get-tuple-element.62.refs_0_) | copy-start | bytes 786436
  64.8 17.3 %all-to-all-start = ((bf16[16,4,16,256]{3,2,1,0:T(8,128)(2,1)}), bf16[16,4,16,256]{3,2,1,0:T(8,128)(2,1)S(1)}, u32[]{:S(2)}, u32[]{:S(2)}) async-start(bf16[16,4,16,256]{3,2,1,0:T(8,128)(2,1)} %get-tuple-element.75), calls=%async_computation | async-start | bytes 1048576 | tf_op jit(solution)/shard_map/all_to_all | solution.py:328
  71.0 11.2 %collective-permute-start.12 = (bf16[128,512]{1,0:T(8,128)(2,1)S(1)}, bf16[128,512]{1,0:T(8,128)(2,1)S(1)}, u32[]{:S(2)}, u32[]{:S(2)}) collective-permute-start(bf16[128,512]{1,0:T(8,128)(2,1)S(1)} %get-tuple-element.59), channel_id=1, source_target_pairs={{0,1},{1,0},{2,3},{3,2},{4,5},{5,4},{6,7},{7,6},{8,9},{9,8},{10,11... | collective-permute-start | bytes 393224 | tf_op jit(solution)/shard_map/ppermute | solution.py:301
  71.6 12.7 %collective-permute-start.13 = (bf16[128,512]{1,0:T(8,128)(2,1)S(1)}, bf16[128,512]{1,0:T(8,128)(2,1)S(1)}, u32[]{:S(2)}, u32[]{:S(2)}) collective-permute-start(bf16[128,512]{1,0:T(8,128)(2,1)S(1)} %get-tuple-element.60), channel_id=1, source_target_pairs={{0,2},{1,3},{2,0},{3,1},{4,6},{5,7},{6,4},{7,5},{8,10},{9,11},{10,... | collective-permute-start | bytes 393224 | tf_op jit(solution)/shard_map/ppermute | solution.py:301
  72.4 14.6 %collective-permute-start.14 = (bf16[128,512]{1,0:T(8,128)(2,1)S(1)}, bf16[128,512]{1,0:T(8,128)(2,1)S(1)}, u32[]{:S(2)}, u32[]{:S(2)}) collective-permute-start(bf16[128,512]{1,0:T(8,128)(2,1)S(1)} %get-tuple-element.61), channel_id=1, source_target_pairs={{0,3},{1,2},{2,1},{3,0},{4,7},{5,6},{6,5},{7,4},{8,11},{9,10},{10,... | collective-permute-start | bytes 393224 | tf_op jit(solution)/shard_map/ppermute | solution.py:301
  73.5 15.3 %collective-permute-start.18 = (bf16[128,768]{1,0:T(8,128)(2,1)S(1)}, bf16[128,768]{1,0:T(8,128)(2,1)S(1)}, u32[]{:S(2)}, u32[]{:S(2)}) collective-permute-start(bf16[128,768]{1,0:T(8,128)(2,1)S(1)} %get-tuple-element.69), channel_id=1, source_target_pairs={{0,1},{1,0},{2,3},{3,2},{4,5},{5,4},{6,7},{7,6},{8,9},{9,8},{10,11... | collective-permute-start | bytes 589832 | tf_op jit(solution)/shard_map/ppermute | solution.py:301
  73.5 16.5 %collective-permute-start.19 = (bf16[128,768]{1,0:T(8,128)(2,1)S(1)}, bf16[128,768]{1,0:T(8,128)(2,1)S(1)}, u32[]{:S(2)}, u32[]{:S(2)}) collective-permute-start(bf16[128,768]{1,0:T(8,128)(2,1)S(1)} %get-tuple-element.70), channel_id=1, source_target_pairs={{0,2},{1,3},{2,0},{3,1},{4,6},{5,7},{6,4},{7,5},{8,10},{9,11},{10,... | collective-permute-start | bytes 589832 | tf_op jit(solution)/shard_map/ppermute | solution.py:301
  82.2 7.8 %collective-permute-start.20 = (bf16[128,768]{1,0:T(8,128)(2,1)S(1)}, bf16[128,768]{1,0:T(8,128)(2,1)S(1)}, u32[]{:S(2)}, u32[]{:S(2)}) collective-permute-start(bf16[128,768]{1,0:T(8,128)(2,1)S(1)} %get-tuple-element.71), channel_id=1, source_target_pairs={{0,3},{1,2},{2,1},{3,0},{4,7},{5,6},{6,5},{7,4},{8,11},{9,10},{10,... | collective-permute-start | bytes 589832 | tf_op jit(solution)/shard_map/ppermute | solution.py:301
  84.3 7.5 %collective-permute-start.23 = (bf16[16,256]{1,0:T(8,128)(2,1)S(1)}, bf16[16,256]{1,0:T(8,128)(2,1)S(1)}, u32[]{:S(2)}, u32[]{:S(2)}) collective-permute-start(bf16[16,256]{1,0:T(8,128)(2,1)S(1)} %get-tuple-element.80), channel_id=1, source_target_pairs={{0,192},{4,196},{8,200},{12,204},{16,208},{20,212},{24,216},{28,22... | collective-permute-start | bytes 24584 | tf_op jit(solution)/shard_map/ppermute | solution.py:308
  86.9 6.4 %collective-permute-start.22 = (bf16[16,256]{1,0:T(8,128)(2,1)S(1)}, bf16[16,256]{1,0:T(8,128)(2,1)S(1)}, u32[]{:S(2)}, u32[]{:S(2)}) collective-permute-start(bf16[16,256]{1,0:T(8,128)(2,1)S(1)} %get-tuple-element.81), channel_id=1, source_target_pairs={{0,128},{4,132},{8,136},{12,140},{16,144},{20,148},{24,152},{28,15... | collective-permute-start | bytes 24584 | tf_op jit(solution)/shard_map/ppermute | solution.py:308
  88.8 4.5 %collective-permute-start.21 = (bf16[16,256]{1,0:T(8,128)(2,1)S(1)}, bf16[16,256]{1,0:T(8,128)(2,1)S(1)}, u32[]{:S(2)}, u32[]{:S(2)}) collective-permute-start(bf16[16,256]{1,0:T(8,128)(2,1)S(1)} %get-tuple-element.79), channel_id=1, source_target_pairs={{0,64},{4,68},{8,72},{12,76},{16,80},{20,84},{24,88},{28,92},{32,9... | collective-permute-start | bytes 24584 | tf_op jit(solution)/shard_map/ppermute | solution.py:308
  90.0 3.4 %copy-start.5 = (f32[16,2,128]{2,1,0:T(2,128)S(1)}, f32[16,2,128]{2,1,0:T(2,128)}, u32[]{:S(2)}) copy-start(f32[16,2,128]{2,1,0:T(2,128)} %param.15) | copy-start | bytes 49156
  93.4 0.7 copy-start.3
  93.4 0.7 copy-start.4

commit v3 on v2

--- a/solution.py
+++ b/solution.py
@@ -34,16 +34,16 @@
 HALVES = 2
 HALF_HEADS = GROUP // HALVES
 HALF = HALF_HEADS * HEAD_WIDTH
-TOGETHER = 2
 ROWS = 256
-CHUNK = 512
+CHUNK = 1024
+WIDE = HALF_HEADS * ROWS
 BLOCKS = SLOT_COUNT // ROWS
 
 bf16 = jnp.bfloat16
 f32 = jnp.float32
 VMEM = pl.BlockSpec(memory_space=pltpu.VMEM)
 SMEM = pl.BlockSpec(memory_space=pltpu.SMEM)
-PARAMS = pltpu.CompilerParams(vmem_limit_bytes=28 * 1024 * 1024)
+PARAMS = pltpu.CompilerParams(vmem_limit_bytes=36 * 1024 * 1024)
 
 
 def nn(a, b):
@@ -124,13 +124,17 @@
 
 
 class Unit:
-    def __init__(self, slot, head, block):
-        self.slot, self.head = slot, head
-        self.first = block * ROWS
+    def __init__(self, slot):
+        self.slot = slot
+        self.first = slot * ROWS
         self.rows = slice(self.first, self.first + ROWS)
         end = PREFIX_TOKENS + self.first + ROWS
         self.spans = [slice(s, min(s + CHUNK, end)) for s in range(0, end, CHUNK)]
         self.tops, self.top, self.total = [], None, None
+
+
+def head_columns(head):
+    return slice(head * HEAD_WIDTH, (head + 1) * HEAD_WIDTH)
 
 
 def attention_kernel(last, length_ref, place_ref, *refs):
@@ -167,11 +171,12 @@
     dvalues[...] = jnp.zeros_like(dvalues)
 
     def prepare(u):
-        q = q_all[u.rows, u.head]
         row_index = u.first + lax.broadcasted_iota(jnp.int32, (ROWS, HEAD_WIDTH), 0)
-        u.q = q
-        u.g = jnp.where(row_index < length, g_all[u.rows, u.head], jnp.zeros((), bf16))
-        u.q_t = turned(q).astype(bf16)
+        zero = jnp.zeros((), bf16)
+        heads = [head_columns(h) for h in range(HALF_HEADS)]
+        u.q = jnp.concatenate([q_all[u.rows, h] for h in heads], 0)
+        u.g = jnp.concatenate([jnp.where(row_index < length, g_all[u.rows, h], zero) for h in heads], 0)
+        u.q_t = turned(u.q).astype(bf16)
         u.g_wide = turned(u.g)
         u.g_t = u.g_wide.astype(bf16)
 
@@ -181,9 +186,9 @@
         masked = PREFIX_TOKENS + u.first
         if span.stop > masked:
             skip = max(span.start, masked) - span.start
-            shape = (span.stop - span.start - skip, ROWS)
+            shape = (span.stop - span.start - skip, WIDE)
             key_pos = span.start + skip - PREFIX_TOKENS + lax.broadcasted_iota(jnp.int32, shape, 0)
-            row_pos = u.first + lax.broadcasted_iota(jnp.int32, shape, 1)
+            row_pos = u.first + jnp.bitwise_and(lax.broadcasted_iota(jnp.int32, shape, 1), ROWS - 1)
             tail = jnp.where(key_pos <= row_pos, scores[skip:], MASKED)
             scores = jnp.concatenate([scores[:skip], tail], 0) if skip else tail
         top = jnp.max(scores, axis=0, keepdims=True)
@@ -198,8 +203,8 @@
     def end_forward(u):
         inverse = 1.0 / u.total
         u.factors = [jnp.exp2((top - u.top) * LOG2_SCALE) * inverse for top in u.tops]
-        u.attended = jnp.zeros((HEAD_WIDTH, ROWS), f32)
-        u.qgrad = jnp.zeros((HEAD_WIDTH, ROWS), f32)
+        u.attended = jnp.zeros((HEAD_WIDTH, WIDE), f32)
+        u.qgrad = jnp.zeros((HEAD_WIDTH, WIDE), f32)
 
     def attend(u, i):
         span = u.spans[i]
@@ -218,28 +223,22 @@
         dkeys[span] += nn(score_grad, u.q)
 
     def end_backward(u):
-        qgrad_all[u.rows, u.head] = (u.qgrad * SCALE).T.astype(bf16)
-
-    def some_heads(step, carry):
-        units = []
-        for h in range(TOGETHER):
-            start = pl.multiple_of((step * TOGETHER + h) * HEAD_WIDTH, HEAD_WIDTH)
-            for block in range(BLOCKS):
-                units.append(Unit(len(units), pl.ds(start, HEAD_WIDTH), block))
-        for u in units:
-            prepare(u)
-        stages = ((forward, end_forward), (attend, end_attend), (backward, end_backward))
-        for t in range(len(units) + len(stages) - 1):
-            live = [(units[t - s], *stages[s]) for s in range(len(stages)) if 0 <= t - s < len(units)]
-            for i in range(max(len(u.spans) for u, _, _ in live)):
-                for u, work, _ in live:
-                    if i < len(u.spans):
-                        work(u, i)
-            for u, _, end in live:
-                end(u)
-        return carry
-
-    lax.fori_loop(0, HALF_HEADS // TOGETHER, some_heads, 0)
+        turned_back = (u.qgrad * SCALE).T.astype(bf16)
+        for h in range(HALF_HEADS):
+            qgrad_all[u.rows, head_columns(h)] = turned_back[h * ROWS : (h + 1) * ROWS]
+
+    units = [Unit(slot) for slot in range(BLOCKS)]
+    for u in units:
+        prepare(u)
+    stages = ((forward, end_forward), (attend, end_attend), (backward, end_backward))
+    for t in range(len(units) + len(stages) - 1):
+        live = [(units[t - s], *stages[s]) for s in range(len(stages)) if 0 <= t - s < len(units)]
+        for i in range(max(len(u.spans) for u, _, _ in live)):
+            for u, work, _ in live:
+                if i < len(u.spans):
+                    work(u, i)
+        for u, _, end in live:
+            end(u)
 
     for peer in range(PEERS):
         rows = pl.ds(part_start(place, peer, OWN_ROWS), OWN_ROWS)
@@ -276,7 +275,7 @@
         out_shape=outs,
         scratch_shapes=[
             half, half, half_t, half_t, total, total,
-            pltpu.VMEM((TOGETHER * BLOCKS, ALL_TOKENS, ROWS), f32),
+            pltpu.VMEM((BLOCKS, ALL_TOKENS, WIDE), f32),
             every, every, every,
         ],
         compiler_params=PARAMS,

time: 95.1 us -> 91.5 us (0.962)
  Pallas kernels: 31.2 us -> 26.5 us
  waiting for transfers between devices: 17.8 us -> 18.8 us
    pallas_call x2, Pallas kernels: 25.6 us -> 21 us  [attention(): pl.pallas_call(functools.partial(attention_kernel, last), in_specs=[SMEM]...]
  transfers between devices with their start and end apart: 25 -> 25, of which waited for: 8 -> 9; matrix products, arithmetic and copies ran while one was open for 1% -> 1% of each run, Pallas kernels for 19% -> 17%
where the time goes in v3:
time: 91.5 us; the launch traced here: 91.1 us
  starting transfers between devices  40.6 us (44%)
  Pallas kernels  26.5 us (29%)
  waiting for transfers between devices  18.8 us (21%)
  other arithmetic  2.07 us (2%)
  local copies, waits for them, and re-layouts  1.72 us (2%)
  between operations  1.44 us (2%)
    ppermute x12, starting transfers between devices, across(): lax.ppermute(part, 'dp', [(i, i ^ k * stride) for i in range(size)])  22.5 us
    pallas_call x2, Pallas kernels, attention(): pl.pallas_call(functools.partial(attention_kernel, last), in_specs=[SMEM]...  21 us
    ppermute x12, starting transfers between devices, exchange(): lax.ppermute(part, 'tensor', [(i, i ^ peer) for i in range(PEERS)])  11.6 us
    all_to_all x1, waiting for transfers between devices, shards(): lax.all_to_all(prefix_part, 'dp', 0, 0, axis_index_groups=IN_PLANE)  8.01 us
    all_to_all x1, starting transfers between devices, shards(): lax.all_to_all(prefix_part, 'dp', 0, 0, axis_index_groups=IN_PLANE)  6.47 us
    ppermute x12, waiting for transfers between devices, across(): lax.ppermute(part, 'dp', [(i, i ^ k * stride) for i in range(size)])  6.03 us
    ppermute x12, waiting for transfers between devices, exchange(): lax.ppermute(part, 'tensor', [(i, i ^ peer) for i in range(PEERS)])  4.72 us
    pallas_call x1, Pallas kernels, outgoing(): pl.pallas_call(outgoing_kernel, in_specs=[SMEM] + [pl.BlockSpec(memory_sp...  3.85 us
  transfers between devices with their start and end apart: 25, of which 9 were waited for; matrix products, arithmetic and copies ran while one was open for 1% of the time, Pallas kernels for 17%

profile of v3, /device:TPU:1, one launch (start us, length us, event | category | flops | bytes accessed | tf_op | source)
XLA Modules:
  0.0 91.1 jit_solution(1704190642865424103)
XLA Ops:
  0.6 0.7 convert_element_type.20
  1.4 3.9 %collective-permute-start = (bf16[16,256]{1,0:T(8,128)(2,1)S(1)}, bf16[16,256]{1,0:T(8,128)(2,1)S(1)}, u32[]{:S(2)}, u32[]{:S(2)}) collective-permute-start(bf16[16,256]{1,0:T(8,128)(2,1)S(1)} %bitcast.17), channel_id=1, source_target_pairs={{0,64},{4,68},{8,72},{12,76},{16,80},{20,84},{24,88},{28,92},{32,9... | collective-permute-start | bytes 24584 | tf_op jit(solution)/shard_map/ppermute | solution.py:307
  5.3 5.1 %collective-permute-start.1 = (bf16[16,256]{1,0:T(8,128)(2,1)S(1)}, bf16[16,256]{1,0:T(8,128)(2,1)S(1)}, u32[]{:S(2)}, u32[]{:S(2)}) collective-permute-start(bf16[16,256]{1,0:T(8,128)(2,1)S(1)} %bitcast.18), channel_id=1, source_target_pairs={{0,128},{4,132},{8,136},{12,140},{16,144},{20,148},{24,152},{28,15... | collective-permute-start | bytes 24584 | tf_op jit(solution)/shard_map/ppermute | solution.py:307
  11.0 3.9 %shard_map.127 = (bf16[128,1280]{1,0:T(8,128)(2,1)}, bf16[128,1280]{1,0:T(8,128)(2,1)}, bf16[128,1280]{1,0:T(8,128)(2,1)}, bf16[128,1280]{1,0:T(8,128)(2,1)}, bf...) custom-call(s32[2]{0:T(128)} %pad_add_fusion.place_ref, ...), custom_call_target="tpu_custom_call" | custom-call | bytes 5000000 | tf_op jit(solution)/shard_map/pallas_call | solution.py:86
  15.0 1.4 %collective-permute-start.6 = (bf16[64,256]{1,0:T(8,128)(2,1)S(1)}, bf16[64,256]{1,0:T(8,128)(2,1)S(1)}, u32[]{:S(2)}, u32[]{:S(2)}) collective-permute-start(bf16[64,256]{1,0:T(8,128)(2,1)S(1)} %get-tuple-element.82), channel_id=1, source_target_pairs={{0,16},{4,20},{8,24},{12,28},{16,0},{20,4},{24,8},{28,12},{32,48},... | collective-permute-start | bytes 98312 | tf_op jit(solution)/shard_map/ppermute | solution.py:307
  16.4 2.7 %collective-permute-start.3 = (bf16[128,1280]{1,0:T(8,128)(2,1)}, bf16[128,1280]{1,0:T(8,128)(2,1)S(1)}, u32[]{:S(2)}, u32[]{:S(2)}) collective-permute-start(bf16[128,1280]{1,0:T(8,128)(2,1)} %get-tuple-element.43), channel_id=1, source_target_pairs={{0,1},{1,0},{2,3},{3,2},{4,5},{5,4},{6,7},{7,6},{8,9},{9,8},{10,11... | collective-permute-start | bytes 983048 | tf_op jit(solution)/shard_map/ppermute | solution.py:300
  19.1 0.7 collective-permute-start.4
  19.8 0.9 collective-permute-start.5
  20.7 2.6 %collective-permute-start.7 = (bf16[64,256]{1,0:T(8,128)(2,1)S(1)}, bf16[64,256]{1,0:T(8,128)(2,1)S(1)}, u32[]{:S(2)}, u32[]{:S(2)}) collective-permute-start(bf16[64,256]{1,0:T(8,128)(2,1)S(1)} %get-tuple-element.82), channel_id=1, source_target_pairs={{0,32},{4,36},{8,40},{12,44},{16,48},{20,52},{24,56},{28,60},{32,0... | collective-permute-start | bytes 98312 | tf_op jit(solution)/shard_map/ppermute | solution.py:307
  23.3 1.6 %collective-permute-done.7 = bf16[64,256]{1,0:T(8,128)(2,1)S(1)} collective-permute-done((bf16[64,256]{1,0:T(8,128)(2,1)S(1)}, bf16[64,256]{1,0:T(8,128)(2,1)S(1)}, u32[]{:S(2)}, u32[]{:S(2)}) %collective-permute-start.7) | collective-permute-done | bytes 32800 | tf_op jit(solution)/shard_map/ppermute | solution.py:307
  25.0 2.3 %collective-permute-done.8 = bf16[64,256]{1,0:T(8,128)(2,1)S(1)} collective-permute-done((bf16[64,256]{1,0:T(8,128)(2,1)S(1)}, bf16[64,256]{1,0:T(8,128)(2,1)S(1)}, u32[]{:S(2)}, u32[]{:S(2)}) %collective-permute-start.8) | collective-permute-done | bytes 32800 | tf_op jit(solution)/shard_map/ppermute | solution.py:307
  27.3 1.2 %collective-permute-start.9 = (bf16[256,256]{1,0:T(8,128)(2,1)S(1)}, bf16[256,256]{1,0:T(8,128)(2,1)S(1)}, u32[]{:S(2)}, u32[]{:S(2)}) collective-permute-start(bf16[256,256]{1,0:T(8,128)(2,1)S(1)} %constant_dynamic-update-slice_fusion.4.refs_8_), channel_id=1, source_target_pairs={{0,4},{4,0},{8,12},{12,8},{16,20},{20,16},{24,28},{28,24},{32,36},... | collective-permute-start | bytes 393224 | tf_op jit(solution)/shard_map/ppermute | solution.py:307
  28.5 2.5 %collective-permute-start.10 = (bf16[256,256]{1,0:T(8,128)(2,1)S(1)}, bf16[256,256]{1,0:T(8,128)(2,1)S(1)}, u32[]{:S(2)}, u32[]{:S(2)}) collective-permute-start(bf16[256,256]{1,0:T(8,128)(2,1)S(1)} %constant_dynamic-update-slice_fusion.4.refs_8_), channel_id=1, source_target_pairs={{0,8},{4,12},{8,0},{12,4},{16,24},{20,28},{24,16},{28,20},{32,40},... | collective-permute-start | bytes 393224 | tf_op jit(solution)/shard_map/ppermute | solution.py:307
  31.8 3.9 %collective-permute-done.5.refs_3_.refs_7_ = bf16[128,1280]{1,0:T(8,128)(2,1)S(1)} collective-permute-done((bf16[128,1280]{1,0:T(8,128)(2,1)}, bf16[128,1280]{1,0:T(8,128)(2,1)S(1)}, u32[]{:S(2)}, u32[]{:S(2)}) %collective-permute-start.5) | collective-permute-done | bytes 327712 | tf_op jit(solution)/shard_map/ppermute | solution.py:300
  36.0 0.7 collective-permute-start.16
  36.8 1.1 %collective-permute-start.17 = (bf16[128,1024]{1,0:T(8,128)(2,1)S(1)}, bf16[128,1024]{1,0:T(8,128)(2,1)S(1)}, u32[]{:S(2)}, u32[]{:S(2)}) collective-permute-start(bf16[128,1024]{1,0:T(8,128)(2,1)S(1)} %copy-done.6), channel_id=1, source_target_pairs={{0,3},{1,2},{2,1},{3,0},{4,7},{5,6},{6,5},{7,4},{8,11},{9,10},{10,... | collective-permute-start | bytes 786440 | tf_op jit(solution)/shard_map/ppermute | solution.py:300
  38.2 1.0 %copy-done.1 = bf16[128,1280]{1,0:T(8,128)(2,1)S(1)} copy-done((bf16[128,1280]{1,0:T(8,128)(2,1)S(1)}, bf16[128,1280]{1,0:T(8,128)(2,1)}, u32[]{:S(2)}) %copy-start.1) | copy-done | bytes 327704
  39.1 9.9 %shard_map.128 = (bf16[128,512]{1,0:T(8,128)(2,1)S(1)}, bf16[128,512]{1,0:T(8,128)(2,1)S(1)}, bf16[128,512]{1,0:T(8,128)(2,1)S(1)}, bf16[128,512]{1,0:T(8,128)(2...) custom-call(s32[1]{0:T(128)S(6)} %copy.26.length_ref, s32[2]{0:T(128)S(1)} %copy-done, ...), custom_call_target="tpu_custom_call" | custom-call | flops 5000000000 | bytes 5000000 | tf_op jit(solution)/shard_map/pallas_call | solution.py:271
  49.1 0.8 collective-permute-done.17.refs_3_
  49.9 11.0 %shard_map.129 = (bf16[128,768]{1,0:T(8,128)(2,1)S(1)}, bf16[128,768]{1,0:T(8,128)(2,1)S(1)}, bf16[128,768]{1,0:T(8,128)(2,1)S(1)}, bf16[128,768]{1,0:T(8,128)(2,1)S(1)}, bf16[16,4,16,256]{3,2,1,0:T(8,128)(2,1)}) custom-call(s32[1]{0:T(128)S(6)} %copy.26.length_ref, s32[2]{0:T(128)S(1)} %copy-done, bf16[128,1024]{1,0:T(8,128)(2,1)S(1)} %copy-done.2, ...), custom_call_target="tpu_custom_call" | custom-call | flops 5000000000 | bytes 5000000 | tf_op jit(solution)/shard_map/pallas_call | solution.py:271
  60.9 6.5 %all-to-all-start = ((bf16[16,4,16,256]{3,2,1,0:T(8,128)(2,1)}), bf16[16,4,16,256]{3,2,1,0:T(8,128)(2,1)S(1)}, u32[]{:S(2)}, u32[]{:S(2)}) async-start(bf16[16,4,16,256]{3,2,1,0:T(8,128)(2,1)} %get-tuple-element.75), calls=%async_computation | async-start | bytes 1048576 | tf_op jit(solution)/shard_map/all_to_all | solution.py:327
  67.8 0.7 collective-permute-start.13
  68.6 1.1 %collective-permute-start.14 = (bf16[128,512]{1,0:T(8,128)(2,1)S(1)}, bf16[128,512]{1,0:T(8,128)(2,1)S(1)}, u32[]{:S(2)}, u32[]{:S(2)}) collective-permute-start(bf16[128,512]{1,0:T(8,128)(2,1)S(1)} %get-tuple-element.61), channel_id=1, source_target_pairs={{0,3},{1,2},{2,1},{3,0},{4,7},{5,6},{6,5},{7,4},{8,11},{9,10},{10,... | collective-permute-start | bytes 393224 | tf_op jit(solution)/shard_map/ppermute | solution.py:300
  69.7 0.7 collective-permute-start.19
  70.4 8.0 %all-to-all-done = bf16[16,4,16,256]{3,2,1,0:T(8,128)(2,1)S(1)} async-done(((bf16[16,4,16,256]{3,2,1,0:T(8,128)(2,1)}), bf16[16,4,16,256]{3,2,1,0:T(8,128)(2,1)S(1)}, u32[]{:S(2)}, u32[]{:S(2)}) %all-to-all-start) | async-done | bytes 524320 | tf_op jit(solution)/shard_map/all_to_all | solution.py:327
  78.5 2.2 %collective-permute-start.20 = (bf16[128,768]{1,0:T(8,128)(2,1)S(1)}, bf16[128,768]{1,0:T(8,128)(2,1)S(1)}, u32[]{:S(2)}, u32[]{:S(2)}) collective-permute-start(bf16[128,768]{1,0:T(8,128)(2,1)S(1)} %get-tuple-element.71), channel_id=1, source_target_pairs={{0,3},{1,2},{2,1},{3,0},{4,7},{5,6},{6,5},{7,4},{8,11},{9,10},{10,... | collective-permute-start | bytes 589832 | tf_op jit(solution)/shard_map/ppermute | solution.py:300
  80.7 2.6 %collective-permute-start.23 = (bf16[16,256]{1,0:T(8,128)(2,1)S(1)}, bf16[16,256]{1,0:T(8,128)(2,1)S(1)}, u32[]{:S(2)}, u32[]{:S(2)}) collective-permute-start(bf16[16,256]{1,0:T(8,128)(2,1)S(1)} %get-tuple-element.80), channel_id=1, source_target_pairs={{0,192},{4,196},{8,200},{12,204},{16,208},{20,212},{24,216},{28,22... | collective-permute-start | bytes 24584 | tf_op jit(solution)/shard_map/ppermute | solution.py:307
  83.3 1.9 %collective-permute-start.22 = (bf16[16,256]{1,0:T(8,128)(2,1)S(1)}, bf16[16,256]{1,0:T(8,128)(2,1)S(1)}, u32[]{:S(2)}, u32[]{:S(2)}) collective-permute-start(bf16[16,256]{1,0:T(8,128)(2,1)S(1)} %get-tuple-element.81), channel_id=1, source_target_pairs={{0,128},{4,132},{8,136},{12,140},{16,144},{20,148},{24,152},{28,15... | collective-permute-start | bytes 24584 | tf_op jit(solution)/shard_map/ppermute | solution.py:307
  85.2 1.2 %collective-permute-start.21 = (bf16[16,256]{1,0:T(8,128)(2,1)S(1)}, bf16[16,256]{1,0:T(8,128)(2,1)S(1)}, u32[]{:S(2)}, u32[]{:S(2)}) collective-permute-start(bf16[16,256]{1,0:T(8,128)(2,1)S(1)} %get-tuple-element.79), channel_id=1, source_target_pairs={{0,64},{4,68},{8,72},{12,76},{16,80},{20,84},{24,88},{28,92},{32,9... | collective-permute-start | bytes 24584 | tf_op jit(solution)/shard_map/ppermute | solution.py:307
  86.4 1.7 %shard_map.130 = (bf16[1,128,4096]{2,1,0:T(8,128)(2,1)}, bf16[1,128,512]{2,1,0:T(8,128)(2,1)}, bf16[1,128,512]{2,1,0:T(8,128)(2,1)}) custom-call(s32[2]{0:T(128)S(1)} %copy-done, bf16[128,512]{1,0:T(8,128)(2,1)S(1)} %get-tuple-element.58.refs_0_, bf16[128,512]{1,0:T(8,128)(2,1)S(1)} %collective-permute-done.12.refs_1_, ...), custom_call_target="tpu_custom_call" | custom-call | bytes 3000000 | tf_op jit(solution)/shard_map/pallas_call | solution.py:116
  88.2 1.5 %collective-permute-done.22 = bf16[16,256]{1,0:T(8,128)(2,1)S(1)} collective-permute-done((bf16[16,256]{1,0:T(8,128)(2,1)S(1)}, bf16[16,256]{1,0:T(8,128)(2,1)S(1)}, u32[]{:S(2)}, u32[]{:S(2)}) %collective-permute-start.22) | collective-permute-done | bytes 8224 | tf_op jit(solution)/shard_map/ppermute | solution.py:307
  90.5 0.7 multiply_subtract_fusion
  (51 shorter events, 3.0 us)
Async XLA Ops:
  1.4 13.5 %collective-permute-start = (bf16[16,256]{1,0:T(8,128)(2,1)S(1)}, bf16[16,256]{1,0:T(8,128)(2,1)S(1)}, u32[]{:S(2)}, u32[]{:S(2)}) collective-permute-start(bf16[16,256]{1,0:T(8,128)(2,1)S(1)} %bitcast.17), channel_id=1, source_target_pairs={{0,64},{4,68},{8,72},{12,76},{16,80},{20,84},{24,88},{28,92},{32,9... | collective-permute-start | bytes 24584 | tf_op jit(solution)/shard_map/ppermute | solution.py:307
  5.3 9.6 %collective-permute-start.1 = (bf16[16,256]{1,0:T(8,128)(2,1)S(1)}, bf16[16,256]{1,0:T(8,128)(2,1)S(1)}, u32[]{:S(2)}, u32[]{:S(2)}) collective-permute-start(bf16[16,256]{1,0:T(8,128)(2,1)S(1)} %bitcast.18), channel_id=1, source_target_pairs={{0,128},{4,132},{8,136},{12,140},{16,144},{20,148},{24,152},{28,15... | collective-permute-start | bytes 24584 | tf_op jit(solution)/shard_map/ppermute | solution.py:307
  10.4 4.6 %collective-permute-start.2 = (bf16[16,256]{1,0:T(8,128)(2,1)S(1)}, bf16[16,256]{1,0:T(8,128)(2,1)S(1)}, u32[]{:S(2)}, u32[]{:S(2)}) collective-permute-start(bf16[16,256]{1,0:T(8,128)(2,1)S(1)} %bitcast.19), channel_id=1, source_target_pairs={{0,192},{4,196},{8,200},{12,204},{16,208},{20,212},{24,216},{28,22... | collective-permute-start | bytes 24584 | tf_op jit(solution)/shard_map/ppermute | solution.py:307
  14.8 21.9 %copy-start.6 = (bf16[128,1024]{1,0:T(8,128)(2,1)S(1)}, bf16[128,1024]{1,0:T(8,128)(2,1)}, u32[]{:S(2)}) copy-start(bf16[128,1024]{1,0:T(8,128)(2,1)} %get-tuple-element.65) | copy-start | bytes 786436
  15.0 8.3 %collective-permute-start.6 = (bf16[64,256]{1,0:T(8,128)(2,1)S(1)}, bf16[64,256]{1,0:T(8,128)(2,1)S(1)}, u32[]{:S(2)}, u32[]{:S(2)}) collective-permute-start(bf16[64,256]{1,0:T(8,128)(2,1)S(1)} %get-tuple-element.82), channel_id=1, source_target_pairs={{0,16},{4,20},{8,24},{12,28},{16,0},{20,4},{24,8},{28,12},{32,48},... | collective-permute-start | bytes 98312 | tf_op jit(solution)/shard_map/ppermute | solution.py:307
  16.4 14.6 %collective-permute-start.3 = (bf16[128,1280]{1,0:T(8,128)(2,1)}, bf16[128,1280]{1,0:T(8,128)(2,1)S(1)}, u32[]{:S(2)}, u32[]{:S(2)}) collective-permute-start(bf16[128,1280]{1,0:T(8,128)(2,1)} %get-tuple-element.43), channel_id=1, source_target_pairs={{0,1},{1,0},{2,3},{3,2},{4,5},{5,4},{6,7},{7,6},{8,9},{9,8},{10,11... | collective-permute-start | bytes 983048 | tf_op jit(solution)/shard_map/ppermute | solution.py:300
  19.1 12.8 %collective-permute-start.4 = (bf16[128,1280]{1,0:T(8,128)(2,1)}, bf16[128,1280]{1,0:T(8,128)(2,1)S(1)}, u32[]{:S(2)}, u32[]{:S(2)}) collective-permute-start(bf16[128,1280]{1,0:T(8,128)(2,1)} %get-tuple-element.44), channel_id=1, source_target_pairs={{0,2},{1,3},{2,0},{3,1},{4,6},{5,7},{6,4},{7,5},{8,10},{9,11},{10,... | collective-permute-start | bytes 983048 | tf_op jit(solution)/shard_map/ppermute | solution.py:300
  19.8 15.9 %collective-permute-start.5 = (bf16[128,1280]{1,0:T(8,128)(2,1)}, bf16[128,1280]{1,0:T(8,128)(2,1)S(1)}, u32[]{:S(2)}, u32[]{:S(2)}) collective-permute-start(bf16[128,1280]{1,0:T(8,128)(2,1)} %get-tuple-element.45), channel_id=1, source_target_pairs={{0,3},{1,2},{2,1},{3,0},{4,7},{5,6},{6,5},{7,4},{8,11},{9,10},{10,... | collective-permute-start | bytes 983048 | tf_op jit(solution)/shard_map/ppermute | solution.py:300
  20.7 4.3 %collective-permute-start.7 = (bf16[64,256]{1,0:T(8,128)(2,1)S(1)}, bf16[64,256]{1,0:T(8,128)(2,1)S(1)}, u32[]{:S(2)}, u32[]{:S(2)}) collective-permute-start(bf16[64,256]{1,0:T(8,128)(2,1)S(1)} %get-tuple-element.82), channel_id=1, source_target_pairs={{0,32},{4,36},{8,40},{12,44},{16,48},{20,52},{24,56},{28,60},{32,0... | collective-permute-start | bytes 98312 | tf_op jit(solution)/shard_map/ppermute | solution.py:307
  23.3 4.0 %collective-permute-start.8 = (bf16[64,256]{1,0:T(8,128)(2,1)S(1)}, bf16[64,256]{1,0:T(8,128)(2,1)S(1)}, u32[]{:S(2)}, u32[]{:S(2)}) collective-permute-start(bf16[64,256]{1,0:T(8,128)(2,1)S(1)} %get-tuple-element.82), channel_id=1, source_target_pairs={{0,48},{4,52},{8,56},{12,60},{16,32},{20,36},{24,40},{28,44},{32,1... | collective-permute-start | bytes 98312 | tf_op jit(solution)/shard_map/ppermute | solution.py:307
  27.3 9.5 %collective-permute-start.9 = (bf16[256,256]{1,0:T(8,128)(2,1)S(1)}, bf16[256,256]{1,0:T(8,128)(2,1)S(1)}, u32[]{:S(2)}, u32[]{:S(2)}) collective-permute-start(bf16[256,256]{1,0:T(8,128)(2,1)S(1)} %constant_dynamic-update-slice_fusion.4.refs_8_), channel_id=1, source_target_pairs={{0,4},{4,0},{8,12},{12,8},{16,20},{20,16},{24,28},{28,24},{32,36},... | collective-permute-start | bytes 393224 | tf_op jit(solution)/shard_map/ppermute | solution.py:307
  28.5 9.4 %collective-permute-start.10 = (bf16[256,256]{1,0:T(8,128)(2,1)S(1)}, bf16[256,256]{1,0:T(8,128)(2,1)S(1)}, u32[]{:S(2)}, u32[]{:S(2)}) collective-permute-start(bf16[256,256]{1,0:T(8,128)(2,1)S(1)} %constant_dynamic-update-slice_fusion.4.refs_8_), channel_id=1, source_target_pairs={{0,8},{4,12},{8,0},{12,4},{16,24},{20,28},{24,16},{28,20},{32,40},... | collective-permute-start | bytes 393224 | tf_op jit(solution)/shard_map/ppermute | solution.py:307
  31.0 7.2 %collective-permute-start.11 = (bf16[256,256]{1,0:T(8,128)(2,1)S(1)}, bf16[256,256]{1,0:T(8,128)(2,1)S(1)}, u32[]{:S(2)}, u32[]{:S(2)}) collective-permute-start(bf16[256,256]{1,0:T(8,128)(2,1)S(1)} %constant_dynamic-update-slice_fusion.4.refs_8_), channel_id=1, source_target_pairs={{0,12},{4,8},{8,4},{12,0},{16,28},{20,24},{24,20},{28,16},{32,44},... | collective-permute-start | bytes 393224 | tf_op jit(solution)/shard_map/ppermute | solution.py:307
  35.7 2.4 %copy-start = (s32[2]{0:T(128)S(1)}, s32[2]{0:T(128)}, u32[]{:S(2)}) copy-start(s32[2]{0:T(128)} %pad_add_fusion.place_ref) | copy-start | bytes 28
  35.7 13.4 %collective-permute-start.15 = (bf16[128,1024]{1,0:T(8,128)(2,1)}, bf16[128,1024]{1,0:T(8,128)(2,1)S(1)}, u32[]{:S(2)}, u32[]{:S(2)}) collective-permute-start(bf16[128,1024]{1,0:T(8,128)(2,1)} %get-tuple-element.63), channel_id=1, source_target_pairs={{0,1},{1,0},{2,3},{3,2},{4,5},{5,4},{6,7},{7,6},{8,9},{9,8},{10,11... | collective-permute-start | bytes 786440 | tf_op jit(solution)/shard_map/ppermute | solution.py:300
  36.0 13.1 %collective-permute-start.16 = (bf16[128,1024]{1,0:T(8,128)(2,1)}, bf16[128,1024]{1,0:T(8,128)(2,1)S(1)}, u32[]{:S(2)}, u32[]{:S(2)}) collective-permute-start(bf16[128,1024]{1,0:T(8,128)(2,1)} %get-tuple-element.64), channel_id=1, source_target_pairs={{0,2},{1,3},{2,0},{3,1},{4,6},{5,7},{6,4},{7,5},{8,10},{9,11},{10,... | collective-permute-start | bytes 786440 | tf_op jit(solution)/shard_map/ppermute | solution.py:300
  36.8 13.1 %collective-permute-start.17 = (bf16[128,1024]{1,0:T(8,128)(2,1)S(1)}, bf16[128,1024]{1,0:T(8,128)(2,1)S(1)}, u32[]{:S(2)}, u32[]{:S(2)}) collective-permute-start(bf16[128,1024]{1,0:T(8,128)(2,1)S(1)} %copy-done.6), channel_id=1, source_target_pairs={{0,3},{1,2},{2,1},{3,0},{4,7},{5,6},{6,5},{7,4},{8,11},{9,10},{10,... | collective-permute-start | bytes 786440 | tf_op jit(solution)/shard_map/ppermute | solution.py:300
  38.2 1.0 %copy-start.1 = (bf16[128,1280]{1,0:T(8,128)(2,1)S(1)}, bf16[128,1280]{1,0:T(8,128)(2,1)}, u32[]{:S(2)}) copy-start(bf16[128,1280]{1,0:T(8,128)(2,1)} %get-tuple-element.50.refs_0_.refs_4_) | copy-start | bytes 983044
  39.1 10.8 %copy-start.2 = (bf16[128,1024]{1,0:T(8,128)(2,1)S(1)}, bf16[128,1024]{1,0:T(8,128)(2,1)}, u32[]{:S(2)}) copy-start(bf16[128,1024]{1,0:T(8,128)(2,1)} %get-tuple-element.62.refs_0_) | copy-start | bytes 786436
  60.9 17.5 %all-to-all-start = ((bf16[16,4,16,256]{3,2,1,0:T(8,128)(2,1)}), bf16[16,4,16,256]{3,2,1,0:T(8,128)(2,1)S(1)}, u32[]{:S(2)}, u32[]{:S(2)}) async-start(bf16[16,4,16,256]{3,2,1,0:T(8,128)(2,1)} %get-tuple-element.75), calls=%async_computation | async-start | bytes 1048576 | tf_op jit(solution)/shard_map/all_to_all | solution.py:327
  67.4 11.1 %collective-permute-start.12 = (bf16[128,512]{1,0:T(8,128)(2,1)S(1)}, bf16[128,512]{1,0:T(8,128)(2,1)S(1)}, u32[]{:S(2)}, u32[]{:S(2)}) collective-permute-start(bf16[128,512]{1,0:T(8,128)(2,1)S(1)} %get-tuple-element.59), channel_id=1, source_target_pairs={{0,1},{1,0},{2,3},{3,2},{4,5},{5,4},{6,7},{7,6},{8,9},{9,8},{10,11... | collective-permute-start | bytes 393224 | tf_op jit(solution)/shard_map/ppermute | solution.py:300
  67.8 12.9 %collective-permute-start.13 = (bf16[128,512]{1,0:T(8,128)(2,1)S(1)}, bf16[128,512]{1,0:T(8,128)(2,1)S(1)}, u32[]{:S(2)}, u32[]{:S(2)}) collective-permute-start(bf16[128,512]{1,0:T(8,128)(2,1)S(1)} %get-tuple-element.60), channel_id=1, source_target_pairs={{0,2},{1,3},{2,0},{3,1},{4,6},{5,7},{6,4},{7,5},{8,10},{9,11},{10,... | collective-permute-start | bytes 393224 | tf_op jit(solution)/shard_map/ppermute | solution.py:300
  68.6 14.7 %collective-permute-start.14 = (bf16[128,512]{1,0:T(8,128)(2,1)S(1)}, bf16[128,512]{1,0:T(8,128)(2,1)S(1)}, u32[]{:S(2)}, u32[]{:S(2)}) collective-permute-start(bf16[128,512]{1,0:T(8,128)(2,1)S(1)} %get-tuple-element.61), channel_id=1, source_target_pairs={{0,3},{1,2},{2,1},{3,0},{4,7},{5,6},{6,5},{7,4},{8,11},{9,10},{10,... | collective-permute-start | bytes 393224 | tf_op jit(solution)/shard_map/ppermute | solution.py:300
  69.6 15.5 %collective-permute-start.18 = (bf16[128,768]{1,0:T(8,128)(2,1)S(1)}, bf16[128,768]{1,0:T(8,128)(2,1)S(1)}, u32[]{:S(2)}, u32[]{:S(2)}) collective-permute-start(bf16[128,768]{1,0:T(8,128)(2,1)S(1)} %get-tuple-element.69), channel_id=1, source_target_pairs={{0,1},{1,0},{2,3},{3,2},{4,5},{5,4},{6,7},{7,6},{8,9},{9,8},{10,11... | collective-permute-start | bytes 589832 | tf_op jit(solution)/shard_map/ppermute | solution.py:300
  69.7 16.7 %collective-permute-start.19 = (bf16[128,768]{1,0:T(8,128)(2,1)S(1)}, bf16[128,768]{1,0:T(8,128)(2,1)S(1)}, u32[]{:S(2)}, u32[]{:S(2)}) collective-permute-start(bf16[128,768]{1,0:T(8,128)(2,1)S(1)} %get-tuple-element.70), channel_id=1, source_target_pairs={{0,2},{1,3},{2,0},{3,1},{4,6},{5,7},{6,4},{7,5},{8,10},{9,11},{10,... | collective-permute-start | bytes 589832 | tf_op jit(solution)/shard_map/ppermute | solution.py:300
  78.5 7.8 %collective-permute-start.20 = (bf16[128,768]{1,0:T(8,128)(2,1)S(1)}, bf16[128,768]{1,0:T(8,128)(2,1)S(1)}, u32[]{:S(2)}, u32[]{:S(2)}) collective-permute-start(bf16[128,768]{1,0:T(8,128)(2,1)S(1)} %get-tuple-element.71), channel_id=1, source_target_pairs={{0,3},{1,2},{2,1},{3,0},{4,7},{5,6},{6,5},{7,4},{8,11},{9,10},{10,... | collective-permute-start | bytes 589832 | tf_op jit(solution)/shard_map/ppermute | solution.py:300
  80.7 7.5 %collective-permute-start.23 = (bf16[16,256]{1,0:T(8,128)(2,1)S(1)}, bf16[16,256]{1,0:T(8,128)(2,1)S(1)}, u32[]{:S(2)}, u32[]{:S(2)}) collective-permute-start(bf16[16,256]{1,0:T(8,128)(2,1)S(1)} %get-tuple-element.80), channel_id=1, source_target_pairs={{0,192},{4,196},{8,200},{12,204},{16,208},{20,212},{24,216},{28,22... | collective-permute-start | bytes 24584 | tf_op jit(solution)/shard_map/ppermute | solution.py:307
  83.3 6.4 %collective-permute-start.22 = (bf16[16,256]{1,0:T(8,128)(2,1)S(1)}, bf16[16,256]{1,0:T(8,128)(2,1)S(1)}, u32[]{:S(2)}, u32[]{:S(2)}) collective-permute-start(bf16[16,256]{1,0:T(8,128)(2,1)S(1)} %get-tuple-element.81), channel_id=1, source_target_pairs={{0,128},{4,132},{8,136},{12,140},{16,144},{20,148},{24,152},{28,15... | collective-permute-start | bytes 24584 | tf_op jit(solution)/shard_map/ppermute | solution.py:307
  85.2 4.5 %collective-permute-start.21 = (bf16[16,256]{1,0:T(8,128)(2,1)S(1)}, bf16[16,256]{1,0:T(8,128)(2,1)S(1)}, u32[]{:S(2)}, u32[]{:S(2)}) collective-permute-start(bf16[16,256]{1,0:T(8,128)(2,1)S(1)} %get-tuple-element.79), channel_id=1, source_target_pairs={{0,64},{4,68},{8,72},{12,76},{16,80},{20,84},{24,88},{28,92},{32,9... | collective-permute-start | bytes 24584 | tf_op jit(solution)/shard_map/ppermute | solution.py:307
  86.4 3.4 %copy-start.5 = (f32[16,2,128]{2,1,0:T(2,128)S(1)}, f32[16,2,128]{2,1,0:T(2,128)}, u32[]{:S(2)}) copy-start(f32[16,2,128]{2,1,0:T(2,128)} %param.15) | copy-start | bytes 49156
  89.7 0.7 copy-start.3
  89.7 0.7 copy-start.4

commit v4 on v3

--- a/solution.py
+++ b/solution.py
@@ -100,7 +100,10 @@
 
 def assemble_kernel(place_ref, *refs):
     first, second = refs[:PEERS], refs[PEERS : 2 * PEERS]
-    q_ref, k_ref, v_ref = refs[2 * PEERS :]
+    c_in, m_in, v_in, q_ref, k_ref, v_ref, c_out, m_out, v_out = refs[2 * PEERS :]
+    c_out[...] = c_in[...]
+    m_out[...] = BETA_ONE * m_in[...]
+    v_out[...] = BETA_TWO * v_in[...]
     place = place_ref[0]
     for peer in range(PEERS):
         heads = part_start(place, peer, GROUP * HEAD_WIDTH)
@@ -111,16 +114,17 @@
         v_ref[0, :, shared] = second[peer][:, HALF + HEAD_WIDTH :]
 
 
-def assemble(place, first, second):
+def assemble(place, first, second, trained):
+    held = [jax.ShapeDtypeStruct(x.shape, f32) for x in trained]
     narrow = jax.ShapeDtypeStruct((1, OWN_ROWS, KEY_VALUE_HEADS * HEAD_WIDTH), bf16)
     return pl.pallas_call(
         assemble_kernel,
-        in_specs=[SMEM] + [VMEM] * (2 * PEERS),
-        out_specs=[VMEM] * 3,
-        out_shape=[jax.ShapeDtypeStruct((1, OWN_ROWS, QUERY_HEADS * HEAD_WIDTH), bf16), narrow, narrow],
+        in_specs=[SMEM] + [VMEM] * (2 * PEERS + 3),
+        out_specs=[VMEM] * 6,
+        out_shape=[jax.ShapeDtypeStruct((1, OWN_ROWS, QUERY_HEADS * HEAD_WIDTH), bf16), narrow, narrow, *held],
         compiler_params=PARAMS,
         cost_estimate=pl.CostEstimate(flops=0, bytes_accessed=3 * 10**6, transcendentals=0),
-    )(place, *first, *second)
+    )(place, *first, *second, *trained)
 
 
 class Unit:
@@ -329,10 +333,12 @@
     plane_sum = jnp.sum(arrived.astype(f32), 0).astype(bf16)
     arrived = across([plane_sum[k] for k in range(PLANES)])
     prefix_grad = sum(part.astype(f32) for part in arrived).reshape(cartridge.shape)
-    q_grad, key_grad, value_grad = assemble(place, first_back, second_back)
-
-    new_m = BETA_ONE * first_moment + (1.0 - BETA_ONE) * prefix_grad
-    new_v = BETA_TWO * second_moment + (1.0 - BETA_TWO) * prefix_grad * prefix_grad
+    q_grad, key_grad, value_grad, cartridge, old_m, old_v = assemble(
+        place, first_back, second_back, (cartridge, first_moment, second_moment)
+    )
+
+    new_m = old_m + (1.0 - BETA_ONE) * prefix_grad
+    new_v = old_v + (1.0 - BETA_TWO) * prefix_grad * prefix_grad
     update = new_m / (1.0 - BETA_ONE**STEP) / (jnp.sqrt(new_v / (1.0 - BETA_TWO**STEP)) + ADAM_EPS)
     new_cartridge = cartridge - LEARN_RATE * update
     return (q_grad, key_grad, value_grad, new_cartridge, new_m, new_v)

time: 91.5 us -> 90.8 us (level)
  transfers between devices with their start and end apart: 25 -> 25, of which waited for: 9 -> 8; matrix products, arithmetic and copies ran while one was open for 1% -> 1% of each run, Pallas kernels for 17% -> 17%
where the time goes in v4:
time: 90.8 us; the launch traced here: 90.5 us
  starting transfers between devices  40.7 us (45%)
  Pallas kernels  26.5 us (29%)
  waiting for transfers between devices  18.7 us (21%)
  other arithmetic  2.07 us (2%)
  between operations  1.44 us (2%)
  local copies, waits for them, and re-layouts  1.04 us (1%)
    ppermute x12, starting transfers between devices, across(): lax.ppermute(part, 'dp', [(i, i ^ k * stride) for i in range(size)])  22.6 us
    pallas_call x2, Pallas kernels, attention(): pl.pallas_call(functools.partial(attention_kernel, last), in_specs=[SMEM]...  21 us
    ppermute x12, starting transfers between devices, exchange(): lax.ppermute(part, 'tensor', [(i, i ^ peer) for i in range(PEERS)])  11.6 us
    all_to_all x1, waiting for transfers between devices, shards(): lax.all_to_all(prefix_part, 'dp', 0, 0, axis_index_groups=IN_PLANE)  8.01 us
    all_to_all x1, starting transfers between devices, shards(): lax.all_to_all(prefix_part, 'dp', 0, 0, axis_index_groups=IN_PLANE)  6.47 us
    ppermute x12, waiting for transfers between devices, across(): lax.ppermute(part, 'dp', [(i, i ^ k * stride) for i in range(size)])  6 us
    ppermute x12, waiting for transfers between devices, exchange(): lax.ppermute(part, 'tensor', [(i, i ^ peer) for i in range(PEERS)])  4.72 us
    pallas_call x1, Pallas kernels, outgoing(): pl.pallas_call(outgoing_kernel, in_specs=[SMEM] + [pl.BlockSpec(memory_sp...  3.85 us
  transfers between devices with their start and end apart: 25, of which 8 were waited for; matrix products, arithmetic and copies ran while one was open for 1% of the time, Pallas kernels for 17%

profile of v4, /device:TPU:1, one launch (start us, length us, event | category | flops | bytes accessed | tf_op | source)
XLA Modules:
  0.0 90.5 jit_solution(8536173607673277743)
XLA Ops:
  0.6 0.7 convert_element_type.20
  1.4 3.9 %collective-permute-start = (bf16[16,256]{1,0:T(8,128)(2,1)S(1)}, bf16[16,256]{1,0:T(8,128)(2,1)S(1)}, u32[]{:S(2)}, u32[]{:S(2)}) collective-permute-start(bf16[16,256]{1,0:T(8,128)(2,1)S(1)} %bitcast.17), channel_id=1, source_target_pairs={{0,64},{4,68},{8,72},{12,76},{16,80},{20,84},{24,88},{28,92},{32,9... | collective-permute-start | bytes 24584 | tf_op jit(solution)/shard_map/ppermute | solution.py:311
  5.3 5.1 %collective-permute-start.1 = (bf16[16,256]{1,0:T(8,128)(2,1)S(1)}, bf16[16,256]{1,0:T(8,128)(2,1)S(1)}, u32[]{:S(2)}, u32[]{:S(2)}) collective-permute-start(bf16[16,256]{1,0:T(8,128)(2,1)S(1)} %bitcast.18), channel_id=1, source_target_pairs={{0,128},{4,132},{8,136},{12,140},{16,144},{20,148},{24,152},{28,15... | collective-permute-start | bytes 24584 | tf_op jit(solution)/shard_map/ppermute | solution.py:311
  11.0 3.9 %shard_map.127 = (bf16[128,1280]{1,0:T(8,128)(2,1)}, bf16[128,1280]{1,0:T(8,128)(2,1)}, bf16[128,1280]{1,0:T(8,128)(2,1)}, bf16[128,1280]{1,0:T(8,128)(2,1)}, bf...) custom-call(s32[2]{0:T(128)} %pad_add_fusion.place_ref, ...), custom_call_target="tpu_custom_call" | custom-call | bytes 5000000 | tf_op jit(solution)/shard_map/pallas_call | solution.py:86
  15.0 1.4 %collective-permute-start.6 = (bf16[64,256]{1,0:T(8,128)(2,1)S(1)}, bf16[64,256]{1,0:T(8,128)(2,1)S(1)}, u32[]{:S(2)}, u32[]{:S(2)}) collective-permute-start(bf16[64,256]{1,0:T(8,128)(2,1)S(1)} %get-tuple-element.88), channel_id=1, source_target_pairs={{0,16},{4,20},{8,24},{12,28},{16,0},{20,4},{24,8},{28,12},{32,48},... | collective-permute-start | bytes 98312 | tf_op jit(solution)/shard_map/ppermute | solution.py:311
  16.4 2.7 %collective-permute-start.3 = (bf16[128,1280]{1,0:T(8,128)(2,1)}, bf16[128,1280]{1,0:T(8,128)(2,1)S(1)}, u32[]{:S(2)}, u32[]{:S(2)}) collective-permute-start(bf16[128,1280]{1,0:T(8,128)(2,1)} %get-tuple-element.46), channel_id=1, source_target_pairs={{0,1},{1,0},{2,3},{3,2},{4,5},{5,4},{6,7},{7,6},{8,9},{9,8},{10,11... | collective-permute-start | bytes 983048 | tf_op jit(solution)/shard_map/ppermute | solution.py:304
  19.1 0.7 collective-permute-start.4
  19.8 0.9 collective-permute-start.5
  20.7 2.6 %collective-permute-start.7 = (bf16[64,256]{1,0:T(8,128)(2,1)S(1)}, bf16[64,256]{1,0:T(8,128)(2,1)S(1)}, u32[]{:S(2)}, u32[]{:S(2)}) collective-permute-start(bf16[64,256]{1,0:T(8,128)(2,1)S(1)} %get-tuple-element.88), channel_id=1, source_target_pairs={{0,32},{4,36},{8,40},{12,44},{16,48},{20,52},{24,56},{28,60},{32,0... | collective-permute-start | bytes 98312 | tf_op jit(solution)/shard_map/ppermute | solution.py:311
  23.3 1.6 %collective-permute-done.7 = bf16[64,256]{1,0:T(8,128)(2,1)S(1)} collective-permute-done((bf16[64,256]{1,0:T(8,128)(2,1)S(1)}, bf16[64,256]{1,0:T(8,128)(2,1)S(1)}, u32[]{:S(2)}, u32[]{:S(2)}) %collective-permute-start.7) | collective-permute-done | bytes 32800 | tf_op jit(solution)/shard_map/ppermute | solution.py:311
  25.0 2.3 %collective-permute-done.8 = bf16[64,256]{1,0:T(8,128)(2,1)S(1)} collective-permute-done((bf16[64,256]{1,0:T(8,128)(2,1)S(1)}, bf16[64,256]{1,0:T(8,128)(2,1)S(1)}, u32[]{:S(2)}, u32[]{:S(2)}) %collective-permute-start.8) | collective-permute-done | bytes 32800 | tf_op jit(solution)/shard_map/ppermute | solution.py:311
  27.3 1.2 %collective-permute-start.9 = (bf16[256,256]{1,0:T(8,128)(2,1)S(1)}, bf16[256,256]{1,0:T(8,128)(2,1)S(1)}, u32[]{:S(2)}, u32[]{:S(2)}) collective-permute-start(bf16[256,256]{1,0:T(8,128)(2,1)S(1)} %constant_dynamic-update-slice_fusion.4.refs_8_), channel_id=1, source_target_pairs={{0,4},{4,0},{8,12},{12,8},{16,20},{20,16},{24,28},{28,24},{32,36},... | collective-permute-start | bytes 393224 | tf_op jit(solution)/shard_map/ppermute | solution.py:311
  28.5 2.5 %collective-permute-start.10 = (bf16[256,256]{1,0:T(8,128)(2,1)S(1)}, bf16[256,256]{1,0:T(8,128)(2,1)S(1)}, u32[]{:S(2)}, u32[]{:S(2)}) collective-permute-start(bf16[256,256]{1,0:T(8,128)(2,1)S(1)} %constant_dynamic-update-slice_fusion.4.refs_8_), channel_id=1, source_target_pairs={{0,8},{4,12},{8,0},{12,4},{16,24},{20,28},{24,16},{28,20},{32,40},... | collective-permute-start | bytes 393224 | tf_op jit(solution)/shard_map/ppermute | solution.py:311
  31.8 3.9 %collective-permute-done.5.refs_3_.refs_7_ = bf16[128,1280]{1,0:T(8,128)(2,1)S(1)} collective-permute-done((bf16[128,1280]{1,0:T(8,128)(2,1)}, bf16[128,1280]{1,0:T(8,128)(2,1)S(1)}, u32[]{:S(2)}, u32[]{:S(2)}) %collective-permute-start.5) | collective-permute-done | bytes 327712 | tf_op jit(solution)/shard_map/ppermute | solution.py:304
  36.0 0.7 collective-permute-start.16
  36.8 1.1 %collective-permute-start.17 = (bf16[128,1024]{1,0:T(8,128)(2,1)S(1)}, bf16[128,1024]{1,0:T(8,128)(2,1)S(1)}, u32[]{:S(2)}, u32[]{:S(2)}) collective-permute-start(bf16[128,1024]{1,0:T(8,128)(2,1)S(1)} %copy-done.6), channel_id=1, source_target_pairs={{0,3},{1,2},{2,1},{3,0},{4,7},{5,6},{6,5},{7,4},{8,11},{9,10},{10,... | collective-permute-start | bytes 786440 | tf_op jit(solution)/shard_map/ppermute | solution.py:304
  38.2 1.0 %copy-done.4 = bf16[128,1280]{1,0:T(8,128)(2,1)S(1)} copy-done((bf16[128,1280]{1,0:T(8,128)(2,1)S(1)}, bf16[128,1280]{1,0:T(8,128)(2,1)}, u32[]{:S(2)}) %copy-start.4) | copy-done | bytes 327704
  39.1 9.9 %shard_map.128 = (bf16[128,512]{1,0:T(8,128)(2,1)S(1)}, bf16[128,512]{1,0:T(8,128)(2,1)S(1)}, bf16[128,512]{1,0:T(8,128)(2,1)S(1)}, bf16[128,512]{1,0:T(8,128)(2...) custom-call(s32[1]{0:T(128)S(6)} %copy.26.length_ref, s32[2]{0:T(128)S(1)} %copy-done.3, ...), custom_call_target="tpu_custom_call" | custom-call | flops 5000000000 | bytes 5000000 | tf_op jit(solution)/shard_map/pallas_call | solution.py:275
  49.1 0.8 collective-permute-done.17.refs_3_
  49.9 11.0 %shard_map.129 = (bf16[128,768]{1,0:T(8,128)(2,1)S(1)}, bf16[128,768]{1,0:T(8,128)(2,1)S(1)}, bf16[128,768]{1,0:T(8,128)(2,1)S(1)}, bf16[128,768]{1,0:T(8,128)(2,1)S(1)}, bf16[16,4,16,256]{3,2,1,0:T(8,128)(2,1)}) custom-call(s32[1]{0:T(128)S(6)} %copy.26.length_ref, s32[2]{0:T(128)S(1)} %copy-done.3, bf16[128,1024]{1,0:T(8,128)(2,1)S(1)} %copy-done.5, ...), custom_call_target="tpu_custom_call" | custom-call | flops 5000000000 | bytes 5000000 | tf_op jit(solution)/shard_map/pallas_call | solution.py:275
  60.9 6.5 %all-to-all-start = ((bf16[16,4,16,256]{3,2,1,0:T(8,128)(2,1)}), bf16[16,4,16,256]{3,2,1,0:T(8,128)(2,1)S(1)}, u32[]{:S(2)}, u32[]{:S(2)}) async-start(bf16[16,4,16,256]{3,2,1,0:T(8,128)(2,1)} %get-tuple-element.80), calls=%async_computation | async-start | bytes 1048576 | tf_op jit(solution)/shard_map/all_to_all | solution.py:331
  67.8 0.7 collective-permute-start.13
  68.6 1.1 %collective-permute-start.14 = (bf16[128,512]{1,0:T(8,128)(2,1)S(1)}, bf16[128,512]{1,0:T(8,128)(2,1)S(1)}, u32[]{:S(2)}, u32[]{:S(2)}) collective-permute-start(bf16[128,512]{1,0:T(8,128)(2,1)S(1)} %get-tuple-element.64), channel_id=1, source_target_pairs={{0,3},{1,2},{2,1},{3,0},{4,7},{5,6},{6,5},{7,4},{8,11},{9,10},{10,... | collective-permute-start | bytes 393224 | tf_op jit(solution)/shard_map/ppermute | solution.py:304
  69.7 0.7 collective-permute-start.19
  70.4 8.0 %all-to-all-done = bf16[16,4,16,256]{3,2,1,0:T(8,128)(2,1)S(1)} async-done(((bf16[16,4,16,256]{3,2,1,0:T(8,128)(2,1)}), bf16[16,4,16,256]{3,2,1,0:T(8,128)(2,1)S(1)}, u32[]{:S(2)}, u32[]{:S(2)}) %all-to-all-start) | async-done | bytes 524320 | tf_op jit(solution)/shard_map/all_to_all | solution.py:331
  78.5 2.2 %collective-permute-start.20 = (bf16[128,768]{1,0:T(8,128)(2,1)S(1)}, bf16[128,768]{1,0:T(8,128)(2,1)S(1)}, u32[]{:S(2)}, u32[]{:S(2)}) collective-permute-start(bf16[128,768]{1,0:T(8,128)(2,1)S(1)} %get-tuple-element.74), channel_id=1, source_target_pairs={{0,3},{1,2},{2,1},{3,0},{4,7},{5,6},{6,5},{7,4},{8,11},{9,10},{10,... | collective-permute-start | bytes 589832 | tf_op jit(solution)/shard_map/ppermute | solution.py:304
  80.7 2.7 %collective-permute-start.23 = (bf16[16,256]{1,0:T(8,128)(2,1)S(1)}, bf16[16,256]{1,0:T(8,128)(2,1)S(1)}, u32[]{:S(2)}, u32[]{:S(2)}) collective-permute-start(bf16[16,256]{1,0:T(8,128)(2,1)S(1)} %get-tuple-element.86), channel_id=1, source_target_pairs={{0,192},{4,196},{8,200},{12,204},{16,208},{20,212},{24,216},{28,22... | collective-permute-start | bytes 24584 | tf_op jit(solution)/shard_map/ppermute | solution.py:311
  83.4 1.9 %collective-permute-start.22 = (bf16[16,256]{1,0:T(8,128)(2,1)S(1)}, bf16[16,256]{1,0:T(8,128)(2,1)S(1)}, u32[]{:S(2)}, u32[]{:S(2)}) collective-permute-start(bf16[16,256]{1,0:T(8,128)(2,1)S(1)} %get-tuple-element.87), channel_id=1, source_target_pairs={{0,128},{4,132},{8,136},{12,140},{16,144},{20,148},{24,152},{28,15... | collective-permute-start | bytes 24584 | tf_op jit(solution)/shard_map/ppermute | solution.py:311
  85.3 1.2 %collective-permute-start.21 = (bf16[16,256]{1,0:T(8,128)(2,1)S(1)}, bf16[16,256]{1,0:T(8,128)(2,1)S(1)}, u32[]{:S(2)}, u32[]{:S(2)}) collective-permute-start(bf16[16,256]{1,0:T(8,128)(2,1)S(1)} %get-tuple-element.85), channel_id=1, source_target_pairs={{0,64},{4,68},{8,72},{12,76},{16,80},{20,84},{24,88},{28,92},{32,9... | collective-permute-start | bytes 24584 | tf_op jit(solution)/shard_map/ppermute | solution.py:311
  86.5 1.7 %shard_map.130 = (bf16[1,128,4096]{2,1,0:T(8,128)(2,1)}, bf16[1,128,512]{2,1,0:T(8,128)(2,1)}, bf16[1,128,512]{2,1,0:T(8,128)(2,1)}, f32[16,2,128]{2,1,0:T(2,128...) custom-call(s32[2]{0:T(128)S(1)} %copy-done.3, bf16[128,512]{1,0:T(8,128)(2,1)S(1)} %get-tuple-element.61.refs_0_, ...), custom_call_target="tpu_custom_call" | custom-call | bytes 3000000 | tf_op jit(solution)/shard_map/pallas_call | solution.py:120
  88.2 1.6 %collective-permute-done.22 = bf16[16,256]{1,0:T(8,128)(2,1)S(1)} collective-permute-done((bf16[16,256]{1,0:T(8,128)(2,1)S(1)}, bf16[16,256]{1,0:T(8,128)(2,1)S(1)}, u32[]{:S(2)}, u32[]{:S(2)}) %collective-permute-start.22) | collective-permute-done | bytes 8224 | tf_op jit(solution)/shard_map/ppermute | solution.py:311
  89.8 0.7 multiply_subtract_fusion
  (51 shorter events, 2.2 us)
Async XLA Ops:
  1.4 13.5 %collective-permute-start = (bf16[16,256]{1,0:T(8,128)(2,1)S(1)}, bf16[16,256]{1,0:T(8,128)(2,1)S(1)}, u32[]{:S(2)}, u32[]{:S(2)}) collective-permute-start(bf16[16,256]{1,0:T(8,128)(2,1)S(1)} %bitcast.17), channel_id=1, source_target_pairs={{0,64},{4,68},{8,72},{12,76},{16,80},{20,84},{24,88},{28,92},{32,9... | collective-permute-start | bytes 24584 | tf_op jit(solution)/shard_map/ppermute | solution.py:311
  5.3 9.6 %collective-permute-start.1 = (bf16[16,256]{1,0:T(8,128)(2,1)S(1)}, bf16[16,256]{1,0:T(8,128)(2,1)S(1)}, u32[]{:S(2)}, u32[]{:S(2)}) collective-permute-start(bf16[16,256]{1,0:T(8,128)(2,1)S(1)} %bitcast.18), channel_id=1, source_target_pairs={{0,128},{4,132},{8,136},{12,140},{16,144},{20,148},{24,152},{28,15... | collective-permute-start | bytes 24584 | tf_op jit(solution)/shard_map/ppermute | solution.py:311
  10.4 4.6 %collective-permute-start.2 = (bf16[16,256]{1,0:T(8,128)(2,1)S(1)}, bf16[16,256]{1,0:T(8,128)(2,1)S(1)}, u32[]{:S(2)}, u32[]{:S(2)}) collective-permute-start(bf16[16,256]{1,0:T(8,128)(2,1)S(1)} %bitcast.19), channel_id=1, source_target_pairs={{0,192},{4,196},{8,200},{12,204},{16,208},{20,212},{24,216},{28,22... | collective-permute-start | bytes 24584 | tf_op jit(solution)/shard_map/ppermute | solution.py:311
  14.8 21.9 %copy-start.6 = (bf16[128,1024]{1,0:T(8,128)(2,1)S(1)}, bf16[128,1024]{1,0:T(8,128)(2,1)}, u32[]{:S(2)}) copy-start(bf16[128,1024]{1,0:T(8,128)(2,1)} %get-tuple-element.68) | copy-start | bytes 786436
  15.0 8.3 %collective-permute-start.6 = (bf16[64,256]{1,0:T(8,128)(2,1)S(1)}, bf16[64,256]{1,0:T(8,128)(2,1)S(1)}, u32[]{:S(2)}, u32[]{:S(2)}) collective-permute-start(bf16[64,256]{1,0:T(8,128)(2,1)S(1)} %get-tuple-element.88), channel_id=1, source_target_pairs={{0,16},{4,20},{8,24},{12,28},{16,0},{20,4},{24,8},{28,12},{32,48},... | collective-permute-start | bytes 98312 | tf_op jit(solution)/shard_map/ppermute | solution.py:311
  16.4 14.6 %collective-permute-start.3 = (bf16[128,1280]{1,0:T(8,128)(2,1)}, bf16[128,1280]{1,0:T(8,128)(2,1)S(1)}, u32[]{:S(2)}, u32[]{:S(2)}) collective-permute-start(bf16[128,1280]{1,0:T(8,128)(2,1)} %get-tuple-element.46), channel_id=1, source_target_pairs={{0,1},{1,0},{2,3},{3,2},{4,5},{5,4},{6,7},{7,6},{8,9},{9,8},{10,11... | collective-permute-start | bytes 983048 | tf_op jit(solution)/shard_map/ppermute | solution.py:304
  19.1 12.8 %collective-permute-start.4 = (bf16[128,1280]{1,0:T(8,128)(2,1)}, bf16[128,1280]{1,0:T(8,128)(2,1)S(1)}, u32[]{:S(2)}, u32[]{:S(2)}) collective-permute-start(bf16[128,1280]{1,0:T(8,128)(2,1)} %get-tuple-element.47), channel_id=1, source_target_pairs={{0,2},{1,3},{2,0},{3,1},{4,6},{5,7},{6,4},{7,5},{8,10},{9,11},{10,... | collective-permute-start | bytes 983048 | tf_op jit(solution)/shard_map/ppermute | solution.py:304
  19.8 15.9 %collective-permute-start.5 = (bf16[128,1280]{1,0:T(8,128)(2,1)}, bf16[128,1280]{1,0:T(8,128)(2,1)S(1)}, u32[]{:S(2)}, u32[]{:S(2)}) collective-permute-start(bf16[128,1280]{1,0:T(8,128)(2,1)} %get-tuple-element.48), channel_id=1, source_target_pairs={{0,3},{1,2},{2,1},{3,0},{4,7},{5,6},{6,5},{7,4},{8,11},{9,10},{10,... | collective-permute-start | bytes 983048 | tf_op jit(solution)/shard_map/ppermute | solution.py:304
  20.7 4.3 %collective-permute-start.7 = (bf16[64,256]{1,0:T(8,128)(2,1)S(1)}, bf16[64,256]{1,0:T(8,128)(2,1)S(1)}, u32[]{:S(2)}, u32[]{:S(2)}) collective-permute-start(bf16[64,256]{1,0:T(8,128)(2,1)S(1)} %get-tuple-element.88), channel_id=1, source_target_pairs={{0,32},{4,36},{8,40},{12,44},{16,48},{20,52},{24,56},{28,60},{32,0... | collective-permute-start | bytes 98312 | tf_op jit(solution)/shard_map/ppermute | solution.py:311
  23.3 4.0 %collective-permute-start.8 = (bf16[64,256]{1,0:T(8,128)(2,1)S(1)}, bf16[64,256]{1,0:T(8,128)(2,1)S(1)}, u32[]{:S(2)}, u32[]{:S(2)}) collective-permute-start(bf16[64,256]{1,0:T(8,128)(2,1)S(1)} %get-tuple-element.88), channel_id=1, source_target_pairs={{0,48},{4,52},{8,56},{12,60},{16,32},{20,36},{24,40},{28,44},{32,1... | collective-permute-start | bytes 98312 | tf_op jit(solution)/shard_map/ppermute | solution.py:311
  27.3 9.5 %collective-permute-start.9 = (bf16[256,256]{1,0:T(8,128)(2,1)S(1)}, bf16[256,256]{1,0:T(8,128)(2,1)S(1)}, u32[]{:S(2)}, u32[]{:S(2)}) collective-permute-start(bf16[256,256]{1,0:T(8,128)(2,1)S(1)} %constant_dynamic-update-slice_fusion.4.refs_8_), channel_id=1, source_target_pairs={{0,4},{4,0},{8,12},{12,8},{16,20},{20,16},{24,28},{28,24},{32,36},... | collective-permute-start | bytes 393224 | tf_op jit(solution)/shard_map/ppermute | solution.py:311
  28.5 9.4 %collective-permute-start.10 = (bf16[256,256]{1,0:T(8,128)(2,1)S(1)}, bf16[256,256]{1,0:T(8,128)(2,1)S(1)}, u32[]{:S(2)}, u32[]{:S(2)}) collective-permute-start(bf16[256,256]{1,0:T(8,128)(2,1)S(1)} %constant_dynamic-update-slice_fusion.4.refs_8_), channel_id=1, source_target_pairs={{0,8},{4,12},{8,0},{12,4},{16,24},{20,28},{24,16},{28,20},{32,40},... | collective-permute-start | bytes 393224 | tf_op jit(solution)/shard_map/ppermute | solution.py:311
  31.0 7.2 %collective-permute-start.11 = (bf16[256,256]{1,0:T(8,128)(2,1)S(1)}, bf16[256,256]{1,0:T(8,128)(2,1)S(1)}, u32[]{:S(2)}, u32[]{:S(2)}) collective-permute-start(bf16[256,256]{1,0:T(8,128)(2,1)S(1)} %constant_dynamic-update-slice_fusion.4.refs_8_), channel_id=1, source_target_pairs={{0,12},{4,8},{8,4},{12,0},{16,28},{20,24},{24,20},{28,16},{32,44},... | collective-permute-start | bytes 393224 | tf_op jit(solution)/shard_map/ppermute | solution.py:311
  35.7 2.4 %copy-start.3 = (s32[2]{0:T(128)S(1)}, s32[2]{0:T(128)}, u32[]{:S(2)}) copy-start(s32[2]{0:T(128)} %pad_add_fusion.place_ref) | copy-start | bytes 28
  35.7 13.4 %collective-permute-start.15 = (bf16[128,1024]{1,0:T(8,128)(2,1)}, bf16[128,1024]{1,0:T(8,128)(2,1)S(1)}, u32[]{:S(2)}, u32[]{:S(2)}) collective-permute-start(bf16[128,1024]{1,0:T(8,128)(2,1)} %get-tuple-element.66), channel_id=1, source_target_pairs={{0,1},{1,0},{2,3},{3,2},{4,5},{5,4},{6,7},{7,6},{8,9},{9,8},{10,11... | collective-permute-start | bytes 786440 | tf_op jit(solution)/shard_map/ppermute | solution.py:304
  36.0 13.1 %collective-permute-start.16 = (bf16[128,1024]{1,0:T(8,128)(2,1)}, bf16[128,1024]{1,0:T(8,128)(2,1)S(1)}, u32[]{:S(2)}, u32[]{:S(2)}) collective-permute-start(bf16[128,1024]{1,0:T(8,128)(2,1)} %get-tuple-element.67), channel_id=1, source_target_pairs={{0,2},{1,3},{2,0},{3,1},{4,6},{5,7},{6,4},{7,5},{8,10},{9,11},{10,... | collective-permute-start | bytes 786440 | tf_op jit(solution)/shard_map/ppermute | solution.py:304
  36.8 13.1 %collective-permute-start.17 = (bf16[128,1024]{1,0:T(8,128)(2,1)S(1)}, bf16[128,1024]{1,0:T(8,128)(2,1)S(1)}, u32[]{:S(2)}, u32[]{:S(2)}) collective-permute-start(bf16[128,1024]{1,0:T(8,128)(2,1)S(1)} %copy-done.6), channel_id=1, source_target_pairs={{0,3},{1,2},{2,1},{3,0},{4,7},{5,6},{6,5},{7,4},{8,11},{9,10},{10,... | collective-permute-start | bytes 786440 | tf_op jit(solution)/shard_map/ppermute | solution.py:304
  38.2 1.0 %copy-start.4 = (bf16[128,1280]{1,0:T(8,128)(2,1)S(1)}, bf16[128,1280]{1,0:T(8,128)(2,1)}, u32[]{:S(2)}) copy-start(bf16[128,1280]{1,0:T(8,128)(2,1)} %get-tuple-element.53.refs_0_.refs_4_) | copy-start | bytes 983044
  39.1 10.8 %copy-start.5 = (bf16[128,1024]{1,0:T(8,128)(2,1)S(1)}, bf16[128,1024]{1,0:T(8,128)(2,1)}, u32[]{:S(2)}) copy-start(bf16[128,1024]{1,0:T(8,128)(2,1)} %get-tuple-element.65.refs_0_) | copy-start | bytes 786436
  60.9 17.5 %all-to-all-start = ((bf16[16,4,16,256]{3,2,1,0:T(8,128)(2,1)}), bf16[16,4,16,256]{3,2,1,0:T(8,128)(2,1)S(1)}, u32[]{:S(2)}, u32[]{:S(2)}) async-start(bf16[16,4,16,256]{3,2,1,0:T(8,128)(2,1)} %get-tuple-element.80), calls=%async_computation | async-start | bytes 1048576 | tf_op jit(solution)/shard_map/all_to_all | solution.py:331
  67.4 11.1 %collective-permute-start.12 = (bf16[128,512]{1,0:T(8,128)(2,1)S(1)}, bf16[128,512]{1,0:T(8,128)(2,1)S(1)}, u32[]{:S(2)}, u32[]{:S(2)}) collective-permute-start(bf16[128,512]{1,0:T(8,128)(2,1)S(1)} %get-tuple-element.62), channel_id=1, source_target_pairs={{0,1},{1,0},{2,3},{3,2},{4,5},{5,4},{6,7},{7,6},{8,9},{9,8},{10,11... | collective-permute-start | bytes 393224 | tf_op jit(solution)/shard_map/ppermute | solution.py:304
  67.8 12.9 %collective-permute-start.13 = (bf16[128,512]{1,0:T(8,128)(2,1)S(1)}, bf16[128,512]{1,0:T(8,128)(2,1)S(1)}, u32[]{:S(2)}, u32[]{:S(2)}) collective-permute-start(bf16[128,512]{1,0:T(8,128)(2,1)S(1)} %get-tuple-element.63), channel_id=1, source_target_pairs={{0,2},{1,3},{2,0},{3,1},{4,6},{5,7},{6,4},{7,5},{8,10},{9,11},{10,... | collective-permute-start | bytes 393224 | tf_op jit(solution)/shard_map/ppermute | solution.py:304
  68.6 14.8 %collective-permute-start.14 = (bf16[128,512]{1,0:T(8,128)(2,1)S(1)}, bf16[128,512]{1,0:T(8,128)(2,1)S(1)}, u32[]{:S(2)}, u32[]{:S(2)}) collective-permute-start(bf16[128,512]{1,0:T(8,128)(2,1)S(1)} %get-tuple-element.64), channel_id=1, source_target_pairs={{0,3},{1,2},{2,1},{3,0},{4,7},{5,6},{6,5},{7,4},{8,11},{9,10},{10,... | collective-permute-start | bytes 393224 | tf_op jit(solution)/shard_map/ppermute | solution.py:304
  69.6 15.6 %collective-permute-start.18 = (bf16[128,768]{1,0:T(8,128)(2,1)S(1)}, bf16[128,768]{1,0:T(8,128)(2,1)S(1)}, u32[]{:S(2)}, u32[]{:S(2)}) collective-permute-start(bf16[128,768]{1,0:T(8,128)(2,1)S(1)} %get-tuple-element.72), channel_id=1, source_target_pairs={{0,1},{1,0},{2,3},{3,2},{4,5},{5,4},{6,7},{7,6},{8,9},{9,8},{10,11... | collective-permute-start | bytes 589832 | tf_op jit(solution)/shard_map/ppermute | solution.py:304
  69.7 16.8 %collective-permute-start.19 = (bf16[128,768]{1,0:T(8,128)(2,1)S(1)}, bf16[128,768]{1,0:T(8,128)(2,1)S(1)}, u32[]{:S(2)}, u32[]{:S(2)}) collective-permute-start(bf16[128,768]{1,0:T(8,128)(2,1)S(1)} %get-tuple-element.73), channel_id=1, source_target_pairs={{0,2},{1,3},{2,0},{3,1},{4,6},{5,7},{6,4},{7,5},{8,10},{9,11},{10,... | collective-permute-start | bytes 589832 | tf_op jit(solution)/shard_map/ppermute | solution.py:304
  78.5 7.9 %collective-permute-start.20 = (bf16[128,768]{1,0:T(8,128)(2,1)S(1)}, bf16[128,768]{1,0:T(8,128)(2,1)S(1)}, u32[]{:S(2)}, u32[]{:S(2)}) collective-permute-start(bf16[128,768]{1,0:T(8,128)(2,1)S(1)} %get-tuple-element.74), channel_id=1, source_target_pairs={{0,3},{1,2},{2,1},{3,0},{4,7},{5,6},{6,5},{7,4},{8,11},{9,10},{10,... | collective-permute-start | bytes 589832 | tf_op jit(solution)/shard_map/ppermute | solution.py:304
  80.7 5.8 %copy-start = (f32[16,2,128]{2,1,0:T(2,128)S(1)}, f32[16,2,128]{2,1,0:T(2,128)}, u32[]{:S(2)}) copy-start(f32[16,2,128]{2,1,0:T(2,128)} %refs_8_.1) | copy-start | bytes 49156
  80.7 5.8 %copy-start.1 = (f32[16,2,128]{2,1,0:T(2,128)S(1)}, f32[16,2,128]{2,1,0:T(2,128)}, u32[]{:S(2)}) copy-start(f32[16,2,128]{2,1,0:T(2,128)} %refs_9_.1) | copy-start | bytes 49156
  80.7 5.8 %copy-start.2 = (f32[16,2,128]{2,1,0:T(2,128)S(1)}, f32[16,2,128]{2,1,0:T(2,128)}, u32[]{:S(2)}) copy-start(f32[16,2,128]{2,1,0:T(2,128)} %refs_10_.1) | copy-start | bytes 49156
  80.7 7.5 %collective-permute-start.23 = (bf16[16,256]{1,0:T(8,128)(2,1)S(1)}, bf16[16,256]{1,0:T(8,128)(2,1)S(1)}, u32[]{:S(2)}, u32[]{:S(2)}) collective-permute-start(bf16[16,256]{1,0:T(8,128)(2,1)S(1)} %get-tuple-element.86), channel_id=1, source_target_pairs={{0,192},{4,196},{8,200},{12,204},{16,208},{20,212},{24,216},{28,22... | collective-permute-start | bytes 24584 | tf_op jit(solution)/shard_map/ppermute | solution.py:311
  83.4 6.4 %collective-permute-start.22 = (bf16[16,256]{1,0:T(8,128)(2,1)S(1)}, bf16[16,256]{1,0:T(8,128)(2,1)S(1)}, u32[]{:S(2)}, u32[]{:S(2)}) collective-permute-start(bf16[16,256]{1,0:T(8,128)(2,1)S(1)} %get-tuple-element.87), channel_id=1, source_target_pairs={{0,128},{4,132},{8,136},{12,140},{16,144},{20,148},{24,152},{28,15... | collective-permute-start | bytes 24584 | tf_op jit(solution)/shard_map/ppermute | solution.py:311
  85.3 4.5 %collective-permute-start.21 = (bf16[16,256]{1,0:T(8,128)(2,1)S(1)}, bf16[16,256]{1,0:T(8,128)(2,1)S(1)}, u32[]{:S(2)}, u32[]{:S(2)}) collective-permute-start(bf16[16,256]{1,0:T(8,128)(2,1)S(1)} %get-tuple-element.85), channel_id=1, source_target_pairs={{0,64},{4,68},{8,72},{12,76},{16,80},{20,84},{24,88},{28,92},{32,9... | collective-permute-start | bytes 24584 | tf_op jit(solution)/shard_map/ppermute | solution.py:311
